TPU v7x, 32 devices: a whole 2x2x4 slice. The times are simulated.
32 devices in a mesh: head: 4 (over x, core), seq: 8 (over z, y).
Axes of the slice: x: 2, y: 2, z: 4, core: 2. Of those that a mesh axis runs over, the one named last changes fastest.
Arguments:
- tokens: bfloat16 [1536, 2304], P('seq'), may hold values from -70 to 70
- cotangent: bfloat16 [3, 1536, 2304], P(None, 'seq'), may hold values from -6 to 6
- doc_lengths: int32 [8], replicated, may hold values from 1 to 1344, as said below
- pad_mask: int32 [1536], P('seq'), may hold values 0 or 1
- gain_attn_in: float32 [2304], replicated, may hold values from 1.2 to 1.8
- gain_attn_out: float32 [2304], replicated, may hold values from 0.1 to 1.9
- gain_mlp_in: float32 [2304], replicated, may hold values from 0.1 to 1.9
- gain_mlp_out: float32 [2304], replicated, may hold values from 0.1 to 1.9
- w_query: bfloat16 [2048, 2304], P('head'), may hold values from -128 to 128
- w_key: bfloat16 [1024, 2304], P('head'), may hold values from -128 to 128
- w_value: bfloat16 [1024, 2304], P('head'), may hold values from -128 to 128
- w_out: bfloat16 [2048, 2304], P('head'), may hold values from -128 to 128
- w_gate: bfloat16 [9216, 2304], P('head'), may hold values from -128 to 128
- w_up: bfloat16 [9216, 2304], P('head'), may hold values from -128 to 128
- w_down: bfloat16 [9216, 2304], P('head'), may hold values from -128 to 128
Outputs:
- activations: bfloat16 [3, 1536, 2304], P(None, 'seq')
- grad_tokens: bfloat16 [1536, 2304], P('seq')
- grad_w_query: float32 [2048, 2304], P(('head', 'seq'))
- grad_w_key: float32 [1024, 2304], P(('head', 'seq'))
- grad_w_value: float32 [1024, 2304], P(('head', 'seq'))
- grad_w_out: float32 [2048, 2304], P(('head', 'seq'))
- grad_w_gate: float32 [9216, 2304], P(('head', 'seq'))
- grad_w_up: float32 [9216, 2304], P(('head', 'seq'))
- grad_w_down: float32 [9216, 2304], P(('head', 'seq'))
- grad_gain_attn_in: float32 [2304], P('seq')
- grad_gain_attn_out: float32 [2304], P('seq')
- grad_gain_mlp_in: float32 [2304], P('seq')
- grad_gain_mlp_out: float32 [2304], P('seq')
Inputs may be any that keep to these rules, and one draw needn't show every extreme that they name: `doc_lengths`: the lengths sum to 1536; exactly one document, neither the first nor the last, has length 1344, and the others share 192 tokens.
All inputs are finite; a program needn't handle non-finite values. No bound on the sum of `pad_mask` on one device may be relied on, other than what follows from the above.
Results may differ from a plain program's by a relative error of at most 0.028.
Values may be sent and summed in bfloat16 or wider, within the bound.
No kernel may reach another device: no remote copies, remote signals or barrier semaphores. Data moves between devices by JAX's collectives and lax.ppermute only.
A program may use at most 320 MiB of HBM per device.

v0:
```python
import math

import jax
import jax.numpy as jnp
from jax import lax
from jax.sharding import PartitionSpec as P

D = 2304
H = 8
HD = 256
FF = 9216
SOFTCAP = 50


NEG_LARGE = -1e30


def for_sending(value):

    def short(part):
        return part.astype(jnp.bfloat16) if part.dtype == jnp.float32 else part

    return jax.tree.map(short, value)


def slice_codes(master, width_bits):
    whole = jnp.clip(jnp.floor(master.astype(jnp.float32)) + 128.0, 0.0, 255.0)
    if width_bits == 8:
        return (whole - 128.0).astype(jnp.bfloat16)
    step = 2.0 ** (8 - width_bits)
    return (jnp.floor(whole / step) * step + step / 2.0 - 128.0).astype(jnp.bfloat16)


def rms_norm(value, gain):
    return value * lax.rsqrt(jnp.mean(value * value, axis=-1, keepdims=True) + 1e-06) * gain


def rotate(value, cosine, sine):
    half = value.shape[-1] // 2
    first = value[..., :half]
    second = value[..., half:]
    return jnp.concatenate(
        [first * cosine - second * sine, second * cosine + first * sine], axis=-1
    )


def doc_info(positions, doc_lengths):
    ends = jnp.cumsum(doc_lengths)
    before = ends[None, :] <= positions[:, None]
    segment = jnp.sum(before.astype(jnp.int32), axis=1)
    offset = jnp.sum(jnp.where(before, doc_lengths[None, :], 0), axis=1)
    return (segment, positions - offset)


def rope_tables(relative):
    freq = jnp.exp(jnp.arange(HD // 2, dtype=jnp.float32) * (-2.0 * math.log(10000.0) / HD))
    angle = relative.astype(jnp.float32)[:, None] * freq[None, :]
    return (jnp.cos(angle), jnp.sin(angle))


def times_rows(left, right):
    return lax.dot_general(
        left, right, (((1,), (1,)), ((), ())), preferred_element_type=jnp.float32
    )


def times_cols(left, right):
    return lax.dot_general(
        left, right, (((0,), (0,)), ((), ())), preferred_element_type=jnp.float32
    )


def product(left, right):
    return jnp.dot(left, right, preferred_element_type=jnp.float32)


def geglu(gate_act, up_act):
    return jax.nn.gelu(gate_act, approximate=True) * up_act


def body(
    tokens,
    cotangent,
    doc_lengths,
    pad_mask,
    gain_attn_in,
    gain_attn_out,
    gain_mlp_in,
    gain_mlp_out,
    w_query,
    w_key,
    w_value,
    w_out,
    w_gate,
    w_up,
    w_down,
):
    row_count = tokens.shape[0]
    positions = lax.axis_index("seq") * row_count + jnp.arange(row_count, dtype=jnp.int32)
    segment, relative = doc_info(positions, doc_lengths)
    cosine, sine = rope_tables(relative)
    cosine = cosine[:, None, :]
    sine = sine[:, None, :]
    group = w_query.shape[0] // HD
    query_pos = jnp.repeat(positions, group)
    query_seg = jnp.repeat(segment, group)
    scale_model = 1.0 / (64.0 * math.sqrt(D))
    scale_heads = 1.0 / (64.0 * math.sqrt(H * HD))
    scale_hidden = 1.0 / (64.0 * math.sqrt(FF))
    root_scale = 1.0 / math.sqrt(HD)
    inputs = tokens.astype(jnp.float32)

    def permitted(key_count, key_valid):
        key_pos = jnp.arange(key_count, dtype=jnp.int32)
        key_seg, _ = doc_info(key_pos, doc_lengths)
        allowed = (query_seg[:, None] == key_seg[None, :]) & (
            key_pos[None, :] <= query_pos[:, None]
        )
        return allowed & ((key_valid[None, :] == 1) | (key_pos[None, :] == query_pos[:, None]))

    outputs = []
    grad_inputs = jnp.zeros_like(inputs)
    totals = None
    for width_index, width_bits in enumerate((8, 4, 2)):
        code_query = slice_codes(w_query, width_bits)
        code_key = slice_codes(w_key, width_bits)
        code_value = slice_codes(w_value, width_bits)
        code_out = slice_codes(w_out, width_bits)
        code_gate = slice_codes(w_gate, width_bits)
        code_up = slice_codes(w_up, width_bits)
        code_down = slice_codes(w_down, width_bits)
        normed, pull_one = jax.vjp(rms_norm, inputs, gain_attn_in)
        normed_b = normed.astype(jnp.bfloat16)
        query_raw = (scale_model * times_rows(normed_b, code_query)).reshape(row_count, group, HD)
        query_flat = (
            rotate(query_raw, cosine, sine).astype(jnp.bfloat16).reshape(row_count * group, HD)
        )
        key_raw = (scale_model * times_rows(normed_b, code_key)).reshape(row_count, 1, HD)
        key_b = rotate(key_raw, cosine, sine).astype(jnp.bfloat16).reshape(row_count, HD)
        value_b = (scale_model * times_rows(normed_b, code_value)).astype(jnp.bfloat16)
        run_peak = jnp.full((row_count * group,), NEG_LARGE, jnp.float32)
        key_piece = lax.all_gather(key_b, "seq", axis=0, tiled=True)
        value_piece = lax.all_gather(value_b, "seq", axis=0, tiled=True)
        attend_key_valid = lax.all_gather(pad_mask, "seq", axis=0, tiled=True)
        attend_allowed = permitted(key_piece.shape[0], attend_key_valid)
        raw_score = times_rows(query_flat, key_piece)
        masked = jnp.where(
            attend_allowed, SOFTCAP * jnp.tanh(raw_score * (root_scale / SOFTCAP)), NEG_LARGE
        )
        new_peak = jnp.maximum(run_peak, jnp.max(masked, axis=1))
        expo = jnp.where(attend_allowed, jnp.exp(masked - new_peak[:, None]), 0.0)
        run_total = jnp.sum(expo, axis=1)
        run_acc = product(expo.astype(jnp.bfloat16), value_piece)
        run_peak, run_total, run_acc = (new_peak, run_total, run_acc)
        context = run_acc / run_total[:, None]
        log_total = run_peak + jnp.log(run_total)
        context_b = context.astype(jnp.bfloat16).reshape(row_count, group * HD)
        attn_out = lax.psum(
            (scale_heads * product(context_b, code_out)).astype(jnp.bfloat16), "head"
        ).astype(jnp.float32)
        branch_attn, pull_two = jax.vjp(rms_norm, attn_out, gain_attn_out)
        middle = inputs + branch_attn
        normed_two, pull_three = jax.vjp(rms_norm, middle, gain_mlp_in)
        normed_two_b = normed_two.astype(jnp.bfloat16)
        gate_act = scale_model * times_rows(normed_two_b, code_gate)
        up_act = scale_model * times_rows(normed_two_b, code_up)
        hidden, pull_glu = jax.vjp(geglu, gate_act, up_act)
        hidden_b = hidden.astype(jnp.bfloat16)
        feed_out = lax.psum(
            (scale_hidden * product(hidden_b, code_down)).astype(jnp.bfloat16), "head"
        ).astype(jnp.float32)
        branch_feed, pull_four = jax.vjp(rms_norm, feed_out, gain_mlp_out)
        outputs.append((middle + branch_feed).astype(jnp.bfloat16))
        grad_out = cotangent[width_index].astype(jnp.float32)
        grad_feed, grad_gain_four = pull_four(grad_out)
        grad_feed_b = grad_feed.astype(jnp.bfloat16)
        grad_hidden = scale_hidden * times_rows(grad_feed_b, code_down)
        term_down = scale_hidden * times_cols(hidden_b, grad_feed_b)
        grad_gate, grad_up = pull_glu(grad_hidden.astype(jnp.bfloat16).astype(jnp.float32))
        grad_gate_b = grad_gate.astype(jnp.bfloat16)
        grad_up_b = grad_up.astype(jnp.bfloat16)
        term_gate = scale_model * times_cols(grad_gate_b, normed_two_b)
        term_up = scale_model * times_cols(grad_up_b, normed_two_b)
        grad_normed_two = lax.psum(
            (scale_model * (product(grad_gate_b, code_gate) + product(grad_up_b, code_up))).astype(
                jnp.bfloat16
            ),
            "head",
        )
        grad_middle_norm, grad_gain_three = pull_three(grad_normed_two.astype(jnp.float32))
        grad_middle = grad_out + grad_middle_norm
        grad_attn, grad_gain_two = pull_two(grad_middle)
        grad_attn_b = grad_attn.astype(jnp.bfloat16)
        grad_context = scale_heads * times_rows(grad_attn_b, code_out)
        term_out = scale_heads * times_cols(context_b, grad_attn_b)
        grad_context_b = grad_context.astype(jnp.bfloat16).reshape(row_count * group, HD)
        row_delta = jnp.sum(grad_context_b.astype(jnp.float32) * context, axis=1)

        def attend_back(piece):
            key_piece, value_piece, key_valid = piece
            key_count = key_piece.shape[0]
            allowed = permitted(key_count, key_valid)
            raw_score = times_rows(query_flat, key_piece)
            bend_score = jnp.tanh(raw_score * (root_scale / SOFTCAP))
            masked = jnp.where(allowed, SOFTCAP * bend_score, NEG_LARGE)
            prob_full = jnp.where(allowed, jnp.exp(masked - log_total[:, None]), 0.0)
            grad_prob = times_rows(grad_context_b, value_piece)
            grad_raw = (
                prob_full
                * (grad_prob - row_delta[:, None])
                * (1.0 - bend_score * bend_score)
                * root_scale
            ).astype(jnp.bfloat16)
            grad_query = product(grad_raw, key_piece)
            key_term = times_cols(grad_raw, query_flat)
            value_term = times_cols(prob_full.astype(jnp.bfloat16), grad_context_b)
            return (grad_query, key_term, value_term)

        grad_query, grad_keys, grad_values = attend_back(
            (
                lax.all_gather(key_b, "seq", axis=0, tiled=True),
                lax.all_gather(value_b, "seq", axis=0, tiled=True),
                lax.all_gather(pad_mask, "seq", axis=0, tiled=True),
            )
        )
        key_sums = (
            lax.psum_scatter(
                grad_keys.astype(jnp.bfloat16), "seq", scatter_dimension=0, tiled=True
            ).astype(jnp.float32),
            lax.psum_scatter(
                grad_values.astype(jnp.bfloat16), "seq", scatter_dimension=0, tiled=True
            ).astype(jnp.float32),
        )
        grad_query_rot = (
            grad_query.astype(jnp.bfloat16).astype(jnp.float32).reshape(row_count, group, HD)
        )
        grad_query_b = (
            rotate(grad_query_rot, cosine, -sine)
            .astype(jnp.bfloat16)
            .reshape(row_count, group * HD)
        )
        grad_key_rot = (
            key_sums[0].astype(jnp.bfloat16).astype(jnp.float32).reshape(row_count, 1, HD)
        )
        grad_key_b = rotate(grad_key_rot, cosine, -sine).astype(jnp.bfloat16).reshape(row_count, HD)
        grad_value_b = key_sums[1].astype(jnp.bfloat16)
        term_query = scale_model * times_cols(grad_query_b, normed_b)
        term_key = scale_model * times_cols(grad_key_b, normed_b)
        term_value = scale_model * times_cols(grad_value_b, normed_b)
        partial_normed = scale_model * (
            product(grad_query_b, code_query)
            + product(grad_key_b, code_key)
            + product(grad_value_b, code_value)
        )
        grad_normed = lax.psum(partial_normed.astype(jnp.bfloat16), "head")
        grad_input_norm, grad_gain_one = pull_one(grad_normed.astype(jnp.float32))
        grad_inputs = grad_inputs + grad_middle + grad_input_norm
        new_terms = (
            term_query,
            term_key,
            term_value,
            term_out,
            term_gate,
            term_up,
            term_down,
            grad_gain_one,
            grad_gain_two,
            grad_gain_three,
            grad_gain_four,
        )
        if totals is None:
            totals = new_terms
        else:
            totals = jax.tree.map(lambda older, newer: older + newer, totals, new_terms)
    totals = jax.tree.map(
        lambda part: part.astype(jnp.float32),
        lax.psum_scatter(for_sending(totals), "seq", scatter_dimension=0, tiled=True),
    )
    return (
        jnp.stack(outputs),
        grad_inputs.astype(jnp.bfloat16),
        totals[0],
        totals[1],
        totals[2],
        totals[3],
        totals[4],
        totals[5],
        totals[6],
        totals[7],
        totals[8],
        totals[9],
        totals[10],
    )


def solution(mesh):
    in_specs = (
        P("seq", None),
        P(None, "seq", None),
        P(),
        P("seq"),
        P(),
        P(),
        P(),
        P(),
        P("head", None),
        P("head", None),
        P("head", None),
        P("head", None),
        P("head", None),
        P("head", None),
        P("head", None),
    )
    out_specs = (
        P(None, "seq", None),
        P("seq", None),
        P(("head", "seq"), None),
        P(("head", "seq"), None),
        P(("head", "seq"), None),
        P(("head", "seq"), None),
        P(("head", "seq"), None),
        P(("head", "seq"), None),
        P(("head", "seq"), None),
        P("seq"),
        P("seq"),
        P("seq"),
        P("seq"),
    )
    return jax.shard_map(body, mesh=mesh, in_specs=in_specs, out_specs=out_specs, check_vma=False)
```

profile of v0, /device:TPU:0, one launch (start us, length us, event | category | flops | bytes accessed | tf_op | source)
XLA Modules:
  0.0 1948.4 jit_solution(15149154289018659124)
XLA Ops:
  25.0 23.6 %all-reduce = s32[1536]{0:T(1024)S(1)} all-reduce(s32[1536]{0:T(1024)S(1)} %dynamic-update-slice), channel_id=1, replica_groups=mesh['head'=4,'seq'=8] {'seq'}, use_global_device_ids=true, to_apply=%add | all-reduce | flops 1536 | bytes 12288
  51.4 32.1 %all_gather.17 = bf16[1536,256]{1,0:T(8,128)(2,1)S(1)} all-gather(bf16[192,256]{1,0:T(8,128)(2,1)S(1)} %pad_maximum_fusion.14), channel_id=1, replica_groups=mesh['head'=4,'seq'=8] {'seq'}, dimensions={0}, use_global_device_ids=true | all-gather | bytes 884736 | tf_op jit(solution)/shard_map/all_gather | solution.py:142
  83.5 32.4 %all_gather.15 = bf16[1536,256]{1,0:T(8,128)(2,1)S(1)} all-gather(bf16[192,256]{1,0:T(8,128)(2,1)S(1)} %pad_maximum_fusion.13), channel_id=1, replica_groups=mesh['head'=4,'seq'=8] {'seq'}, dimensions={0}, use_global_device_ids=true | all-gather | bytes 884736 | tf_op jit(solution)/shard_map/all_gather | solution.py:142
  115.9 31.9 %all_gather.37 = bf16[1536,256]{1,0:T(8,128)(2,1)S(1)} all-gather(bf16[192,256]{1,0:T(8,128)(2,1)S(1)} %pad_maximum_fusion.15), channel_id=1, replica_groups=mesh['head'=4,'seq'=8] {'seq'}, dimensions={0}, use_global_device_ids=true | all-gather | bytes 884736 | tf_op jit(solution)/shard_map/all_gather | solution.py:142
  147.9 34.1 %all_gather.16 = bf16[1536,256]{1,0:T(8,128)(2,1)} all-gather(bf16[192,256]{1,0:T(8,128)(2,1)S(1)} %fusion.212), channel_id=1, replica_groups=mesh['head'=4,'seq'=8] {'seq'}, dimensions={0}, use_global_device_ids=true | all-gather | bytes 884736 | tf_op jit(solution)/shard_map/all_gather | solution.py:143
  182.0 32.6 %all_gather.38 = bf16[1536,256]{1,0:T(8,128)(2,1)S(1)} all-gather(bf16[192,256]{1,0:T(8,128)(2,1)S(1)} %fusion.214), channel_id=1, replica_groups=mesh['head'=4,'seq'=8] {'seq'}, dimensions={0}, use_global_device_ids=true | all-gather | bytes 884736 | tf_op jit(solution)/shard_map/all_gather | solution.py:143
  214.6 33.6 %all_gather.36 = bf16[1536,256]{1,0:T(8,128)(2,1)} all-gather(bf16[192,256]{1,0:T(8,128)(2,1)S(1)} %fusion.213), channel_id=1, replica_groups=mesh['head'=4,'seq'=8] {'seq'}, dimensions={0}, use_global_device_ids=true | all-gather | bytes 884736 | tf_op jit(solution)/shard_map/all_gather | solution.py:143
  278.5 59.3 %all-reduce.21.cloned.1.call-done = (bf16[192,2304]{1,0:T(8,128)(2,1)}, bf16[192,2304]{1,0:T(8,128)(2,1)}, bf16[192,2304]{1,0:T(8,128)(2,1)}) async-done(((bf16[192,2304]{1,0:T(8,128)(2,1)}, bf16[192,2304]{1,0:T(8,128)(2,1)}, bf16[192,2304]{1,0:T(8,128)(2,1)}), (bf16[192,2304]{1,0:T(8,128)(2,1)}, bf16[192,2304]{1,0:T(8,128)(2,1)}, bf16[192,2304]{1,0:T(8,128)(2,1)})) %all-reduce.21.cloned.1.call-update) | async-done | bytes 2654224 | tf_op jit(solution)/shard_map/psum | solution.py:158
  418.5 61.0 %all-reduce.19.cloned.1.call-done = (bf16[192,2304]{1,0:T(8,128)(2,1)}, bf16[192,2304]{1,0:T(8,128)(2,1)}, bf16[192,2304]{1,0:T(8,128)(2,1)}) async-done(((bf16[192,2304]{1,0:T(8,128)(2,1)}, bf16[192,2304]{1,0:T(8,128)(2,1)}, bf16[192,2304]{1,0:T(8,128)(2,1)}), (bf16[192,2304]{1,0:T(8,128)(2,1)}, bf16[192,2304]{1,0:T(8,128)(2,1)}, bf16[192,2304]{1,0:T(8,128)(2,1)})) %all-reduce.19.cloned.1.call-update) | async-done | bytes 2654224 | tf_op jit(solution)/shard_map/psum | solution.py:169
  485.7 12.7 multiply_convert_fusion
  498.5 11.3 fusion.93
  518.4 11.5 fusion.92
  571.3 59.6 %all-reduce.17.cloned.1.call-done = (bf16[192,2304]{1,0:T(8,128)(2,1)}, bf16[192,2304]{1,0:T(8,128)(2,1)}, bf16[192,2304]{1,0:T(8,128)(2,1)}) async-done(((bf16[192,2304]{1,0:T(8,128)(2,1)}, bf16[192,2304]{1,0:T(8,128)(2,1)}, bf16[192,2304]{1,0:T(8,128)(2,1)}), (bf16[192,2304]{1,0:T(8,128)(2,1)}, bf16[192,2304]{1,0:T(8,128)(2,1)}, bf16[192,2304]{1,0:T(8,128)(2,1)})) %all-reduce.17.cloned.1.call-update) | async-done | bytes 2654224 | tf_op jit(solution)/shard_map/psum | solution.py:184
  725.4 63.0 %reduce-scatter.14.cloned.1.call-done = bf16[192,256]{1,0:T(8,128)(2,1)} async-done(((bf16[1536,256]{1,0:T(8,128)(2,1)}), bf16[192,256]{1,0:T(8,128)(2,1)}) %reduce-scatter.14.cloned.1.call-update) | async-done | bytes 98320 | tf_op jit(solution)/shard_map/reduce_scatter | solution.py:227
  789.3 63.8 %reduce-scatter.22.cloned.1.call-done = bf16[192,256]{1,0:T(8,128)(2,1)} async-done(((bf16[1536,256]{1,0:T(8,128)(2,1)}), bf16[192,256]{1,0:T(8,128)(2,1)}) %reduce-scatter.22.cloned.1.call-update) | async-done | bytes 98320 | tf_op jit(solution)/shard_map/reduce_scatter | solution.py:227
  857.7 61.1 %reduce-scatter.16.cloned.1.call-done = bf16[192,256]{1,0:T(8,128)(2,1)} async-done(((bf16[1536,256]{1,0:T(8,128)(2,1)}), bf16[192,256]{1,0:T(8,128)(2,1)}) %reduce-scatter.16.cloned.1.call-update) | async-done | bytes 98320 | tf_op jit(solution)/shard_map/reduce_scatter | solution.py:230
  924.7 59.0 %reduce-scatter.20.cloned.1.call-done = bf16[192,256]{1,0:T(8,128)(2,1)} async-done(((bf16[1536,256]{1,0:T(8,128)(2,1)}), bf16[192,256]{1,0:T(8,128)(2,1)}) %reduce-scatter.20.cloned.1.call-update) | async-done | bytes 98320 | tf_op jit(solution)/shard_map/reduce_scatter | solution.py:230
  989.7 59.1 %reduce-scatter.24.cloned.1.call-done = bf16[192,256]{1,0:T(8,128)(2,1)} async-done(((bf16[1536,256]{1,0:T(8,128)(2,1)}), bf16[192,256]{1,0:T(8,128)(2,1)}) %reduce-scatter.24.cloned.1.call-update) | async-done | bytes 98320 | tf_op jit(solution)/shard_map/reduce_scatter | solution.py:230
  1064.2 11.8 fusion.553
  1080.7 18.1 convolution_add_fusion.1
  1098.8 14.8 fusion.5
  1123.9 13.8 convolution_add_fusion.3
  1137.7 12.7 fusion.4
  1150.7 10.2 fusion.587
  1160.9 13.9 convolution_add_fusion.5
  1174.8 12.2 fusion.3
  1198.5 36.4 %all-reduce.5 = (bf16[2304]{0:T(1024)(128)(2,1)}, bf16[2304]{0:T(1024)(128)(2,1)}, bf16[2304]{0:T(1024)(128)(2,1)}, bf16[2304]{0:T(1024)(128)(2,1)}) all-reduce(bf16[2304]{0:T(1024)(128)(2,1)} %add_convert_fusion.98, bf16[2304]{0:T(1024)(128)(2,1)} %add_convert_fusion.97, ...), channel_id=15, replica_groups=mesh['head'=4,'seq'=8] {'seq'}, use_global_device_ids=true, to_apply=%region_63.64.clone | all-reduce | flops 9216 | bytes 36864
  1249.9 69.1 %reduce-scatter.32.cloned.1.call-done = bf16[64,2304]{1,0:T(8,128)(2,1)} async-done(((bf16[512,2304]{1,0:T(8,128)(2,1)}), bf16[64,2304]{1,0:T(8,128)(2,1)}) %reduce-scatter.32.cloned.1.call-update) | async-done | bytes 294928 | tf_op jit(solution)/shard_map/reduce_scatter | solution.py:277
  1320.8 70.2 %reduce-scatter.26.cloned.1.call-done = bf16[64,2304]{1,0:T(8,128)(2,1)} async-done(((bf16[512,2304]{1,0:T(8,128)(2,1)}), bf16[64,2304]{1,0:T(8,128)(2,1)}) %reduce-scatter.26.cloned.1.call-update) | async-done | bytes 294928 | tf_op jit(solution)/shard_map/reduce_scatter | solution.py:277
  1392.8 180.6 %reduce-scatter.38.cloned.1.call-done = bf16[288,2304]{1,0:T(8,128)(2,1)} async-done(((bf16[2304,2304]{1,0:T(8,128)(2,1)}), bf16[288,2304]{1,0:T(8,128)(2,1)}) %reduce-scatter.38.cloned.1.call-update) | async-done | bytes 1327120 | tf_op jit(solution)/shard_map/reduce_scatter | solution.py:277
  1576.4 179.9 %reduce-scatter.36.cloned.1.call-done = bf16[288,2304]{1,0:T(8,128)(2,1)} async-done(((bf16[2304,2304]{1,0:T(8,128)(2,1)}), bf16[288,2304]{1,0:T(8,128)(2,1)}) %reduce-scatter.36.cloned.1.call-update) | async-done | bytes 1327120 | tf_op jit(solution)/shard_map/reduce_scatter | solution.py:277
  1759.4 179.3 %reduce-scatter.34.cloned.1.call-done = bf16[288,2304]{1,0:T(8,128)(2,1)} async-done(((bf16[2304,2304]{1,0:T(8,128)(2,1)}), bf16[288,2304]{1,0:T(8,128)(2,1)}) %reduce-scatter.34.cloned.1.call-update) | async-done | bytes 1327120 | tf_op jit(solution)/shard_map/reduce_scatter | solution.py:277
  (630 shorter events, 365.2 us)
Async XLA Ops:
  7.2 330.7 %all-reduce.21.cloned.1.call-start = ((), (), s32[]{:S(2)}) async-start(), calls=%async_computation.29 | async-start | bytes 5308416 | tf_op jit(solution)/shard_map/psum | solution.py:158
  23.2 241.3 %copy-start.119 = (s32[1536]{0:T(1024)}, s32[1536]{0:T(1024)S(1)}, u32[]{:S(2)}) copy-start(s32[1536]{0:T(1024)S(1)} %convert_reduce_fusion) | copy-start | bytes 18436
  48.5 216.0 %copy-start.147 = (pred[1536]{0:T(1024)(128)(4,1)}, pred[1536]{0:T(1024)(128)(4,1)S(1)}, u32[]{:S(2)}) copy-start(pred[1536]{0:T(1024)(128)(4,1)S(1)} %broadcast_compare_fusion) | copy-start | bytes 4612
  48.8 215.7 %copy-start.149 = (s32[384]{0:T(512)}, s32[384]{0:T(512)S(1)}, u32[]{:S(2)}) copy-start(s32[384]{0:T(512)S(1)} %eq.13) | copy-start | bytes 4612
  49.0 215.5 %copy-start.151 = (s32[384]{0:T(512)}, s32[384]{0:T(512)S(1)}, u32[]{:S(2)}) copy-start(s32[384]{0:T(512)S(1)} %le.29) | copy-start | bytes 4612
  50.9 197.3 %copy-start.71 = (f32[192,128]{1,0:T(8,128)}, f32[192,128]{1,0:T(8,128)S(1)}, u32[]{:S(2)}) copy-start(f32[192,128]{1,0:T(8,128)S(1)} %get-tuple-element.136) | copy-start | bytes 294916
  83.5 167.5 %copy-start.43 = (bf16[1536,256]{1,0:T(8,128)(2,1)}, bf16[1536,256]{1,0:T(8,128)(2,1)S(1)}, u32[]{:S(2)}) copy-start(bf16[1536,256]{1,0:T(8,128)(2,1)S(1)} %all_gather.17) | copy-start | bytes 2359300
  115.9 133.0 %copy-start.42 = (bf16[1536,256]{1,0:T(8,128)(2,1)}, bf16[1536,256]{1,0:T(8,128)(2,1)S(1)}, u32[]{:S(2)}) copy-start(bf16[1536,256]{1,0:T(8,128)(2,1)S(1)} %all_gather.15) | copy-start | bytes 2359300
  147.9 102.6 %copy-start.28 = (bf16[1536,256]{1,0:T(8,128)(2,1)}, bf16[1536,256]{1,0:T(8,128)(2,1)S(1)}, u32[]{:S(2)}) copy-start(bf16[1536,256]{1,0:T(8,128)(2,1)S(1)} %all_gather.37) | copy-start | bytes 2359300
  278.5 201.0 %all-reduce.19.cloned.1.call-start = ((), (), s32[]{:S(2)}) async-start(), calls=%async_computation.28 | async-start | bytes 5308416 | tf_op jit(solution)/shard_map/psum | solution.py:169
  418.4 64.4 %copy-start.8 = (bf16[3,192,2304]{2,1,0:T(8,128)(2,1)S(1)}, bf16[3,192,2304]{2,1,0:T(8,128)(2,1)}, u32[]{:S(2)}) copy-start(bf16[3,192,2304]{2,1,0:T(8,128)(2,1)} %param.16) | copy-start | bytes 7962628
  418.4 64.4 %copy-start.89 = (f32[2304]{0:T(1024)S(1)}, f32[2304]{0:T(1024)}, u32[]{:S(2)}) copy-start(f32[2304]{0:T(1024)} %param.22) | copy-start | bytes 27652
  418.4 212.5 %all-reduce.17.cloned.1.call-start = ((), (), s32[]{:S(2)}) async-start(), calls=%async_computation.27 | async-start | bytes 5308416 | tf_op jit(solution)/shard_map/psum | solution.py:184
  563.7 67.2 %copy-start.7 = (bf16[192,2304]{1,0:T(8,128)(2,1)S(1)}, bf16[192,2304]{1,0:T(8,128)(2,1)}, u32[]{:S(2)}) copy-start(bf16[192,2304]{1,0:T(8,128)(2,1)} %get-tuple-element.74) | copy-start | bytes 2654212
  569.8 154.5 %reduce-scatter.18.cloned.1.call-start = ((), (), s32[]{:S(2)}) async-start(), calls=%async_computation.15 | async-start | bytes 884736 | tf_op jit(solution)/shard_map/reduce_scatter | solution.py:227
  660.6 127.7 %reduce-scatter.14.cloned.1.call-start = ((), (), s32[]{:S(2)}) async-start(), calls=%async_computation.13 | async-start | bytes 884736 | tf_op jit(solution)/shard_map/reduce_scatter | solution.py:227
  670.4 182.7 %reduce-scatter.22.cloned.1.call-start = ((), (), s32[]{:S(2)}) async-start(), calls=%async_computation.17 | async-start | bytes 884736 | tf_op jit(solution)/shard_map/reduce_scatter | solution.py:227
  683.9 235.0 %reduce-scatter.16.cloned.1.call-start = ((), (), s32[]{:S(2)}) async-start(), calls=%async_computation.14 | async-start | bytes 884736 | tf_op jit(solution)/shard_map/reduce_scatter | solution.py:230
  692.9 290.8 %reduce-scatter.20.cloned.1.call-start = ((), (), s32[]{:S(2)}) async-start(), calls=%async_computation.16 | async-start | bytes 884736 | tf_op jit(solution)/shard_map/reduce_scatter | solution.py:230
  709.7 339.2 %reduce-scatter.24.cloned.1.call-start = ((), (), s32[]{:S(2)}) async-start(), calls=%async_computation.18 | async-start | bytes 884736 | tf_op jit(solution)/shard_map/reduce_scatter | solution.py:230
  721.2 132.8 %copy-start.129 = (f32[192]{0:T(256)S(1)}, f32[192]{0:T(256)}, u32[]{:S(2)}) copy-start(f32[192]{0:T(256)} %copy-done.128) | copy-start | bytes 2308
  721.2 132.9 %copy-start.162 = (f32[128]{0:T(128)S(1)}, f32[128]{0:T(128)}, u32[]{:S(2)}) copy-start(f32[128]{0:T(128)} %copy-done.161) | copy-start | bytes 1540
  724.0 130.5 %copy-start.52 = (f32[192,2304]{1,0:T(8,128)S(1)}, f32[192,2304]{1,0:T(8,128)}, u32[]{:S(2)}) copy-start(f32[192,2304]{1,0:T(8,128)} %fusion.177) | copy-start | bytes 5308420
  724.1 469.6 %all-reduce.15.cloned.1.call-start = ((), (), s32[]{:S(2)}) async-start(), calls=%async_computation.26 | async-start | bytes 5308416 | tf_op jit(solution)/shard_map/psum | solution.py:255
  857.7 64.8 %copy-start.67 = (bf16[256,2304]{1,0:T(8,128)(2,1)S(1)}, bf16[256,2304]{1,0:T(8,128)(2,1)}, u32[]{:S(2)}) copy-start(bf16[256,2304]{1,0:T(8,128)(2,1)} %param.24) | copy-start | bytes 3538948
  1052.6 194.0 %reduce-scatter.30.cloned.1.call-start = ((), (), s32[]{:S(2)}) async-start(), calls=%async_computation.21 | async-start | bytes 1327104 | tf_op jit(solution)/shard_map/reduce_scatter | solution.py:277
  1056.6 191.6 %reduce-scatter.28.cloned.1.call-start = ((), (), s32[]{:S(2)}) async-start(), calls=%async_computation.20 | async-start | bytes 1327104 | tf_op jit(solution)/shard_map/reduce_scatter | solution.py:277
  1059.5 259.5 %reduce-scatter.32.cloned.1.call-start = ((), (), s32[]{:S(2)}) async-start(), calls=%async_computation.22 | async-start | bytes 2654208 | tf_op jit(solution)/shard_map/reduce_scatter | solution.py:277
  1064.2 326.8 %reduce-scatter.26.cloned.1.call-start = ((), (), s32[]{:S(2)}) async-start(), calls=%async_computation.19 | async-start | bytes 2654208 | tf_op jit(solution)/shard_map/reduce_scatter | solution.py:277
  1080.2 493.2 %reduce-scatter.38.cloned.1.call-start = ((), (), s32[]{:S(2)}) async-start(), calls=%async_computation.25 | async-start | bytes 11943936 | tf_op jit(solution)/shard_map/reduce_scatter | solution.py:277
  1113.6 642.7 %reduce-scatter.36.cloned.1.call-start = ((), (), s32[]{:S(2)}) async-start(), calls=%async_computation.24 | async-start | bytes 11943936 | tf_op jit(solution)/shard_map/reduce_scatter | solution.py:277
  1150.5 788.2 %reduce-scatter.34.cloned.1.call-start = ((), (), s32[]{:S(2)}) async-start(), calls=%async_computation.23 | async-start | bytes 11943936 | tf_op jit(solution)/shard_map/reduce_scatter | solution.py:277
  (188 other events, 1838.4 us)
Sparse Core Ops, SparseCore 0:
  278.6 59.1 all-reduce.20
  418.5 60.8 all-reduce.18
  569.9 60.8 all-reduce.16
  660.7 62.5 reduce-scatter.17
  726.8 61.4 reduce-scatter.13
  791.5 61.5 reduce-scatter.21
  857.3 61.4 reduce-scatter.15
  922.2 61.4 reduce-scatter.19
  987.4 61.4 reduce-scatter.23
  1052.7 59.7 all-reduce.14
  1115.9 64.1 reduce-scatter.29
  1183.9 62.9 reduce-scatter.27
  1251.0 67.9 reduce-scatter.31
  1322.9 68.0 reduce-scatter.25
  1394.4 178.9 reduce-scatter.37
  1577.3 179.0 reduce-scatter.35
  1759.8 178.8 reduce-scatter.33
where the time goes:
time: 1950 us
  waiting for transfers between devices  1170 us (60%)
  matrix products  395 us (20%)
  blocking collectives  257 us (13%)
  other arithmetic  83.4 us (4%)
  local copies, waits for them, and re-layouts  27.9 us (1%)
    reduce_scatter x7, waiting for transfers between devices, body(): lax.psum_scatter(for_sending(totals), 'seq', scatter_dimension=0, tiled=T...  679 us
    reduce_scatter x3, waiting for transfers between devices, body(): lax.psum_scatter(grad_values.astype(jnp.bfloat16), 'seq', scatter_dimensi...  179 us
    dot_general x27, matrix products, times_cols(): lax.dot_general(left, right, (((0,), (0,)), ((), ())), preferred_element_...  144 us
    dot_general x27, matrix products, product(): return jnp.dot(left, right, preferred_element_type=jnp.float32)  135 us
    reduce_scatter x3, waiting for transfers between devices, body(): lax.psum_scatter(grad_keys.astype(jnp.bfloat16), 'seq', scatter_dimension...  127 us
    dot_general x27, matrix products, times_rows(): lax.dot_general(left, right, (((1,), (1,)), ((), ())), preferred_element_...  116 us
    all_gather x3, blocking collectives, body(): value_piece = lax.all_gather(value_b, 'seq', axis=0, tiled=True)  100 us
    all_gather x3, blocking collectives, body(): key_piece = lax.all_gather(key_b, 'seq', axis=0, tiled=True)  96.4 us
  transfers between devices with their start and end apart: 17, of which 13 were waited for; matrix products, arithmetic and copies ran while one was open for 13% of the time, Pallas kernels for 0%

commit v1 on v0

--- a/solution.py
+++ b/solution.py
@@ -45,7 +45,8 @@
 
 
 def doc_info(positions, doc_lengths):
-    ends = jnp.cumsum(doc_lengths)
+    slots = jnp.arange(doc_lengths.shape[0], dtype=jnp.int32)
+    ends = jnp.sum(jnp.where(slots[:, None] <= slots[None, :], doc_lengths[:, None], 0), axis=0)
     before = ends[None, :] <= positions[:, None]
     segment = jnp.sum(before.astype(jnp.int32), axis=1)
     offset = jnp.sum(jnp.where(before, doc_lengths[None, :], 0), axis=1)

time: 1950 us -> 1950 us (level)
  no operation moved by 1% of the time
where the time goes in v1:
time: 1950 us
  waiting for transfers between devices  1170 us (60%)
  matrix products  395 us (20%)
  blocking collectives  257 us (13%)
  other arithmetic  83.3 us (4%)
  local copies, waits for them, and re-layouts  27.9 us (1%)
    reduce_scatter x7, waiting for transfers between devices, body(): lax.psum_scatter(for_sending(totals), 'seq', scatter_dimension=0, tiled=T...  680 us
    reduce_scatter x3, waiting for transfers between devices, body(): lax.psum_scatter(grad_values.astype(jnp.bfloat16), 'seq', scatter_dimensi...  179 us
    dot_general x27, matrix products, times_cols(): lax.dot_general(left, right, (((0,), (0,)), ((), ())), preferred_element_...  144 us
    dot_general x27, matrix products, product(): return jnp.dot(left, right, preferred_element_type=jnp.float32)  135 us
    reduce_scatter x3, waiting for transfers between devices, body(): lax.psum_scatter(grad_keys.astype(jnp.bfloat16), 'seq', scatter_dimension...  127 us
    dot_general x27, matrix products, times_rows(): lax.dot_general(left, right, (((1,), (1,)), ((), ())), preferred_element_...  116 us
    all_gather x3, blocking collectives, body(): value_piece = lax.all_gather(value_b, 'seq', axis=0, tiled=True)  100 us
    all_gather x3, blocking collectives, body(): key_piece = lax.all_gather(key_b, 'seq', axis=0, tiled=True)  96.4 us
  transfers between devices with their start and end apart: 17, of which 13 were waited for; matrix products, arithmetic and copies ran while one was open for 13% of the time, Pallas kernels for 0%

profile of v1, /device:TPU:0, one launch (start us, length us, event | category | flops | bytes accessed | tf_op | source)
XLA Modules:
  0.0 1948.6 jit_solution(11936657946480289037)
XLA Ops:
  24.9 23.6 %all-reduce = s32[1536]{0:T(1024)S(1)} all-reduce(s32[1536]{0:T(1024)S(1)} %dynamic-update-slice), channel_id=1, replica_groups=mesh['head'=4,'seq'=8] {'seq'}, use_global_device_ids=true, to_apply=%add | all-reduce | flops 1536 | bytes 12288
  51.3 32.1 %all_gather.17 = bf16[1536,256]{1,0:T(8,128)(2,1)S(1)} all-gather(bf16[192,256]{1,0:T(8,128)(2,1)S(1)} %pad_maximum_fusion.14), channel_id=1, replica_groups=mesh['head'=4,'seq'=8] {'seq'}, dimensions={0}, use_global_device_ids=true | all-gather | bytes 884736 | tf_op jit(solution)/shard_map/all_gather | solution.py:143
  83.4 32.4 %all_gather.15 = bf16[1536,256]{1,0:T(8,128)(2,1)S(1)} all-gather(bf16[192,256]{1,0:T(8,128)(2,1)S(1)} %pad_maximum_fusion.13), channel_id=1, replica_groups=mesh['head'=4,'seq'=8] {'seq'}, dimensions={0}, use_global_device_ids=true | all-gather | bytes 884736 | tf_op jit(solution)/shard_map/all_gather | solution.py:143
  115.8 31.9 %all_gather.37 = bf16[1536,256]{1,0:T(8,128)(2,1)S(1)} all-gather(bf16[192,256]{1,0:T(8,128)(2,1)S(1)} %pad_maximum_fusion.15), channel_id=1, replica_groups=mesh['head'=4,'seq'=8] {'seq'}, dimensions={0}, use_global_device_ids=true | all-gather | bytes 884736 | tf_op jit(solution)/shard_map/all_gather | solution.py:143
  147.8 34.1 %all_gather.16 = bf16[1536,256]{1,0:T(8,128)(2,1)} all-gather(bf16[192,256]{1,0:T(8,128)(2,1)S(1)} %fusion.212), channel_id=1, replica_groups=mesh['head'=4,'seq'=8] {'seq'}, dimensions={0}, use_global_device_ids=true | all-gather | bytes 884736 | tf_op jit(solution)/shard_map/all_gather | solution.py:144
  181.8 32.6 %all_gather.38 = bf16[1536,256]{1,0:T(8,128)(2,1)S(1)} all-gather(bf16[192,256]{1,0:T(8,128)(2,1)S(1)} %fusion.214), channel_id=1, replica_groups=mesh['head'=4,'seq'=8] {'seq'}, dimensions={0}, use_global_device_ids=true | all-gather | bytes 884736 | tf_op jit(solution)/shard_map/all_gather | solution.py:144
  214.4 33.6 %all_gather.36 = bf16[1536,256]{1,0:T(8,128)(2,1)} all-gather(bf16[192,256]{1,0:T(8,128)(2,1)S(1)} %fusion.213), channel_id=1, replica_groups=mesh['head'=4,'seq'=8] {'seq'}, dimensions={0}, use_global_device_ids=true | all-gather | bytes 884736 | tf_op jit(solution)/shard_map/all_gather | solution.py:144
  278.4 59.3 %all-reduce.21.cloned.1.call-done = (bf16[192,2304]{1,0:T(8,128)(2,1)}, bf16[192,2304]{1,0:T(8,128)(2,1)}, bf16[192,2304]{1,0:T(8,128)(2,1)}) async-done(((bf16[192,2304]{1,0:T(8,128)(2,1)}, bf16[192,2304]{1,0:T(8,128)(2,1)}, bf16[192,2304]{1,0:T(8,128)(2,1)}), (bf16[192,2304]{1,0:T(8,128)(2,1)}, bf16[192,2304]{1,0:T(8,128)(2,1)}, bf16[192,2304]{1,0:T(8,128)(2,1)})) %all-reduce.21.cloned.1.call-update) | async-done | bytes 2654224 | tf_op jit(solution)/shard_map/psum | solution.py:159
  418.4 61.0 %all-reduce.19.cloned.1.call-done = (bf16[192,2304]{1,0:T(8,128)(2,1)}, bf16[192,2304]{1,0:T(8,128)(2,1)}, bf16[192,2304]{1,0:T(8,128)(2,1)}) async-done(((bf16[192,2304]{1,0:T(8,128)(2,1)}, bf16[192,2304]{1,0:T(8,128)(2,1)}, bf16[192,2304]{1,0:T(8,128)(2,1)}), (bf16[192,2304]{1,0:T(8,128)(2,1)}, bf16[192,2304]{1,0:T(8,128)(2,1)}, bf16[192,2304]{1,0:T(8,128)(2,1)})) %all-reduce.19.cloned.1.call-update) | async-done | bytes 2654224 | tf_op jit(solution)/shard_map/psum | solution.py:170
  485.6 12.7 multiply_convert_fusion
  498.3 11.3 fusion.93
  518.3 11.5 fusion.92
  571.2 59.6 %all-reduce.17.cloned.1.call-done = (bf16[192,2304]{1,0:T(8,128)(2,1)}, bf16[192,2304]{1,0:T(8,128)(2,1)}, bf16[192,2304]{1,0:T(8,128)(2,1)}) async-done(((bf16[192,2304]{1,0:T(8,128)(2,1)}, bf16[192,2304]{1,0:T(8,128)(2,1)}, bf16[192,2304]{1,0:T(8,128)(2,1)}), (bf16[192,2304]{1,0:T(8,128)(2,1)}, bf16[192,2304]{1,0:T(8,128)(2,1)}, bf16[192,2304]{1,0:T(8,128)(2,1)})) %all-reduce.17.cloned.1.call-update) | async-done | bytes 2654224 | tf_op jit(solution)/shard_map/psum | solution.py:185
  725.3 63.0 %reduce-scatter.14.cloned.1.call-done = bf16[192,256]{1,0:T(8,128)(2,1)} async-done(((bf16[1536,256]{1,0:T(8,128)(2,1)}), bf16[192,256]{1,0:T(8,128)(2,1)}) %reduce-scatter.14.cloned.1.call-update) | async-done | bytes 98320 | tf_op jit(solution)/shard_map/reduce_scatter | solution.py:228
  789.2 63.8 %reduce-scatter.22.cloned.1.call-done = bf16[192,256]{1,0:T(8,128)(2,1)} async-done(((bf16[1536,256]{1,0:T(8,128)(2,1)}), bf16[192,256]{1,0:T(8,128)(2,1)}) %reduce-scatter.22.cloned.1.call-update) | async-done | bytes 98320 | tf_op jit(solution)/shard_map/reduce_scatter | solution.py:228
  857.6 61.1 %reduce-scatter.16.cloned.1.call-done = bf16[192,256]{1,0:T(8,128)(2,1)} async-done(((bf16[1536,256]{1,0:T(8,128)(2,1)}), bf16[192,256]{1,0:T(8,128)(2,1)}) %reduce-scatter.16.cloned.1.call-update) | async-done | bytes 98320 | tf_op jit(solution)/shard_map/reduce_scatter | solution.py:231
  924.6 59.0 %reduce-scatter.20.cloned.1.call-done = bf16[192,256]{1,0:T(8,128)(2,1)} async-done(((bf16[1536,256]{1,0:T(8,128)(2,1)}), bf16[192,256]{1,0:T(8,128)(2,1)}) %reduce-scatter.20.cloned.1.call-update) | async-done | bytes 98320 | tf_op jit(solution)/shard_map/reduce_scatter | solution.py:231
  989.6 59.1 %reduce-scatter.24.cloned.1.call-done = bf16[192,256]{1,0:T(8,128)(2,1)} async-done(((bf16[1536,256]{1,0:T(8,128)(2,1)}), bf16[192,256]{1,0:T(8,128)(2,1)}) %reduce-scatter.24.cloned.1.call-update) | async-done | bytes 98320 | tf_op jit(solution)/shard_map/reduce_scatter | solution.py:231
  1064.1 11.8 fusion.553
  1080.6 18.1 convolution_add_fusion.1
  1098.7 14.8 fusion.5
  1123.8 13.8 convolution_add_fusion.3
  1137.6 12.7 fusion.4
  1150.6 10.2 fusion.587
  1160.8 13.9 convolution_add_fusion.5
  1174.6 12.2 fusion.3
  1198.4 36.4 %all-reduce.5 = (bf16[2304]{0:T(1024)(128)(2,1)}, bf16[2304]{0:T(1024)(128)(2,1)}, bf16[2304]{0:T(1024)(128)(2,1)}, bf16[2304]{0:T(1024)(128)(2,1)}) all-reduce(bf16[2304]{0:T(1024)(128)(2,1)} %add_convert_fusion.98, bf16[2304]{0:T(1024)(128)(2,1)} %add_convert_fusion.97, ...), channel_id=15, replica_groups=mesh['head'=4,'seq'=8] {'seq'}, use_global_device_ids=true, to_apply=%region_63.64.clone | all-reduce | flops 9216 | bytes 36864
  1249.8 69.3 %reduce-scatter.32.cloned.1.call-done = bf16[64,2304]{1,0:T(8,128)(2,1)} async-done(((bf16[512,2304]{1,0:T(8,128)(2,1)}), bf16[64,2304]{1,0:T(8,128)(2,1)}) %reduce-scatter.32.cloned.1.call-update) | async-done | bytes 294928 | tf_op jit(solution)/shard_map/reduce_scatter | solution.py:278
  1320.9 70.3 %reduce-scatter.26.cloned.1.call-done = bf16[64,2304]{1,0:T(8,128)(2,1)} async-done(((bf16[512,2304]{1,0:T(8,128)(2,1)}), bf16[64,2304]{1,0:T(8,128)(2,1)}) %reduce-scatter.26.cloned.1.call-update) | async-done | bytes 294928 | tf_op jit(solution)/shard_map/reduce_scatter | solution.py:278
  1393.1 180.5 %reduce-scatter.38.cloned.1.call-done = bf16[288,2304]{1,0:T(8,128)(2,1)} async-done(((bf16[2304,2304]{1,0:T(8,128)(2,1)}), bf16[288,2304]{1,0:T(8,128)(2,1)}) %reduce-scatter.38.cloned.1.call-update) | async-done | bytes 1327120 | tf_op jit(solution)/shard_map/reduce_scatter | solution.py:278
  1576.6 179.8 %reduce-scatter.36.cloned.1.call-done = bf16[288,2304]{1,0:T(8,128)(2,1)} async-done(((bf16[2304,2304]{1,0:T(8,128)(2,1)}), bf16[288,2304]{1,0:T(8,128)(2,1)}) %reduce-scatter.36.cloned.1.call-update) | async-done | bytes 1327120 | tf_op jit(solution)/shard_map/reduce_scatter | solution.py:278
  1759.4 179.6 %reduce-scatter.34.cloned.1.call-done = bf16[288,2304]{1,0:T(8,128)(2,1)} async-done(((bf16[2304,2304]{1,0:T(8,128)(2,1)}), bf16[288,2304]{1,0:T(8,128)(2,1)}) %reduce-scatter.34.cloned.1.call-update) | async-done | bytes 1327120 | tf_op jit(solution)/shard_map/reduce_scatter | solution.py:278
  (630 shorter events, 365.1 us)
Async XLA Ops:
  7.2 330.6 %all-reduce.21.cloned.1.call-start = ((), (), s32[]{:S(2)}) async-start(), calls=%async_computation.29 | async-start | bytes 5308416 | tf_op jit(solution)/shard_map/psum | solution.py:159
  23.1 241.3 %copy-start.119 = (s32[1536]{0:T(1024)}, s32[1536]{0:T(1024)S(1)}, u32[]{:S(2)}) copy-start(s32[1536]{0:T(1024)S(1)} %convert_reduce_fusion) | copy-start | bytes 18436
  48.4 216.0 %copy-start.147 = (pred[1536]{0:T(1024)(128)(4,1)}, pred[1536]{0:T(1024)(128)(4,1)S(1)}, u32[]{:S(2)}) copy-start(pred[1536]{0:T(1024)(128)(4,1)S(1)} %broadcast_compare_fusion) | copy-start | bytes 4612
  48.7 215.7 %copy-start.149 = (s32[384]{0:T(512)}, s32[384]{0:T(512)S(1)}, u32[]{:S(2)}) copy-start(s32[384]{0:T(512)S(1)} %eq.13) | copy-start | bytes 4612
  48.9 215.5 %copy-start.151 = (s32[384]{0:T(512)}, s32[384]{0:T(512)S(1)}, u32[]{:S(2)}) copy-start(s32[384]{0:T(512)S(1)} %le.38) | copy-start | bytes 4612
  50.8 197.3 %copy-start.71 = (f32[192,128]{1,0:T(8,128)}, f32[192,128]{1,0:T(8,128)S(1)}, u32[]{:S(2)}) copy-start(f32[192,128]{1,0:T(8,128)S(1)} %get-tuple-element.136) | copy-start | bytes 294916
  83.4 167.5 %copy-start.43 = (bf16[1536,256]{1,0:T(8,128)(2,1)}, bf16[1536,256]{1,0:T(8,128)(2,1)S(1)}, u32[]{:S(2)}) copy-start(bf16[1536,256]{1,0:T(8,128)(2,1)S(1)} %all_gather.17) | copy-start | bytes 2359300
  115.8 133.0 %copy-start.42 = (bf16[1536,256]{1,0:T(8,128)(2,1)}, bf16[1536,256]{1,0:T(8,128)(2,1)S(1)}, u32[]{:S(2)}) copy-start(bf16[1536,256]{1,0:T(8,128)(2,1)S(1)} %all_gather.15) | copy-start | bytes 2359300
  147.8 102.6 %copy-start.28 = (bf16[1536,256]{1,0:T(8,128)(2,1)}, bf16[1536,256]{1,0:T(8,128)(2,1)S(1)}, u32[]{:S(2)}) copy-start(bf16[1536,256]{1,0:T(8,128)(2,1)S(1)} %all_gather.37) | copy-start | bytes 2359300
  278.4 201.0 %all-reduce.19.cloned.1.call-start = ((), (), s32[]{:S(2)}) async-start(), calls=%async_computation.28 | async-start | bytes 5308416 | tf_op jit(solution)/shard_map/psum | solution.py:170
  418.3 64.4 %copy-start.8 = (bf16[3,192,2304]{2,1,0:T(8,128)(2,1)S(1)}, bf16[3,192,2304]{2,1,0:T(8,128)(2,1)}, u32[]{:S(2)}) copy-start(bf16[3,192,2304]{2,1,0:T(8,128)(2,1)} %param.16) | copy-start | bytes 7962628
  418.3 64.4 %copy-start.89 = (f32[2304]{0:T(1024)S(1)}, f32[2304]{0:T(1024)}, u32[]{:S(2)}) copy-start(f32[2304]{0:T(1024)} %param.22) | copy-start | bytes 27652
  418.3 212.4 %all-reduce.17.cloned.1.call-start = ((), (), s32[]{:S(2)}) async-start(), calls=%async_computation.27 | async-start | bytes 5308416 | tf_op jit(solution)/shard_map/psum | solution.py:185
  563.6 67.2 %copy-start.7 = (bf16[192,2304]{1,0:T(8,128)(2,1)S(1)}, bf16[192,2304]{1,0:T(8,128)(2,1)}, u32[]{:S(2)}) copy-start(bf16[192,2304]{1,0:T(8,128)(2,1)} %get-tuple-element.74) | copy-start | bytes 2654212
  569.7 154.5 %reduce-scatter.18.cloned.1.call-start = ((), (), s32[]{:S(2)}) async-start(), calls=%async_computation.15 | async-start | bytes 884736 | tf_op jit(solution)/shard_map/reduce_scatter | solution.py:228
  660.5 127.7 %reduce-scatter.14.cloned.1.call-start = ((), (), s32[]{:S(2)}) async-start(), calls=%async_computation.13 | async-start | bytes 884736 | tf_op jit(solution)/shard_map/reduce_scatter | solution.py:228
  670.3 182.7 %reduce-scatter.22.cloned.1.call-start = ((), (), s32[]{:S(2)}) async-start(), calls=%async_computation.17 | async-start | bytes 884736 | tf_op jit(solution)/shard_map/reduce_scatter | solution.py:228
  683.8 235.0 %reduce-scatter.16.cloned.1.call-start = ((), (), s32[]{:S(2)}) async-start(), calls=%async_computation.14 | async-start | bytes 884736 | tf_op jit(solution)/shard_map/reduce_scatter | solution.py:231
  692.8 290.8 %reduce-scatter.20.cloned.1.call-start = ((), (), s32[]{:S(2)}) async-start(), calls=%async_computation.16 | async-start | bytes 884736 | tf_op jit(solution)/shard_map/reduce_scatter | solution.py:231
  709.5 339.2 %reduce-scatter.24.cloned.1.call-start = ((), (), s32[]{:S(2)}) async-start(), calls=%async_computation.18 | async-start | bytes 884736 | tf_op jit(solution)/shard_map/reduce_scatter | solution.py:231
  721.1 132.8 %copy-start.129 = (f32[192]{0:T(256)S(1)}, f32[192]{0:T(256)}, u32[]{:S(2)}) copy-start(f32[192]{0:T(256)} %copy-done.128) | copy-start | bytes 2308
  721.1 132.9 %copy-start.162 = (f32[128]{0:T(128)S(1)}, f32[128]{0:T(128)}, u32[]{:S(2)}) copy-start(f32[128]{0:T(128)} %copy-done.161) | copy-start | bytes 1540
  723.9 130.5 %copy-start.52 = (f32[192,2304]{1,0:T(8,128)S(1)}, f32[192,2304]{1,0:T(8,128)}, u32[]{:S(2)}) copy-start(f32[192,2304]{1,0:T(8,128)} %fusion.177) | copy-start | bytes 5308420
  724.0 469.6 %all-reduce.15.cloned.1.call-start = ((), (), s32[]{:S(2)}) async-start(), calls=%async_computation.26 | async-start | bytes 5308416 | tf_op jit(solution)/shard_map/psum | solution.py:256
  857.6 64.8 %copy-start.67 = (bf16[256,2304]{1,0:T(8,128)(2,1)S(1)}, bf16[256,2304]{1,0:T(8,128)(2,1)}, u32[]{:S(2)}) copy-start(bf16[256,2304]{1,0:T(8,128)(2,1)} %param.24) | copy-start | bytes 3538948
  1052.5 194.0 %reduce-scatter.30.cloned.1.call-start = ((), (), s32[]{:S(2)}) async-start(), calls=%async_computation.21 | async-start | bytes 1327104 | tf_op jit(solution)/shard_map/reduce_scatter | solution.py:278
  1056.5 191.6 %reduce-scatter.28.cloned.1.call-start = ((), (), s32[]{:S(2)}) async-start(), calls=%async_computation.20 | async-start | bytes 1327104 | tf_op jit(solution)/shard_map/reduce_scatter | solution.py:278
  1059.4 259.7 %reduce-scatter.32.cloned.1.call-start = ((), (), s32[]{:S(2)}) async-start(), calls=%async_computation.22 | async-start | bytes 2654208 | tf_op jit(solution)/shard_map/reduce_scatter | solution.py:278
  1064.1 327.2 %reduce-scatter.26.cloned.1.call-start = ((), (), s32[]{:S(2)}) async-start(), calls=%async_computation.19 | async-start | bytes 2654208 | tf_op jit(solution)/shard_map/reduce_scatter | solution.py:278
  1080.1 493.4 %reduce-scatter.38.cloned.1.call-start = ((), (), s32[]{:S(2)}) async-start(), calls=%async_computation.25 | async-start | bytes 11943936 | tf_op jit(solution)/shard_map/reduce_scatter | solution.py:278
  1113.6 642.8 %reduce-scatter.36.cloned.1.call-start = ((), (), s32[]{:S(2)}) async-start(), calls=%async_computation.24 | async-start | bytes 11943936 | tf_op jit(solution)/shard_map/reduce_scatter | solution.py:278
  1150.4 788.6 %reduce-scatter.34.cloned.1.call-start = ((), (), s32[]{:S(2)}) async-start(), calls=%async_computation.23 | async-start | bytes 11943936 | tf_op jit(solution)/shard_map/reduce_scatter | solution.py:278
  (188 other events, 1838.1 us)
Sparse Core Ops, SparseCore 0:
  278.5 59.1 all-reduce.20
  418.4 60.8 all-reduce.18
  569.8 60.8 all-reduce.16
  660.6 62.5 reduce-scatter.17
  726.7 61.4 reduce-scatter.13
  791.4 61.5 reduce-scatter.21
  857.2 61.4 reduce-scatter.15
  922.1 61.4 reduce-scatter.19
  987.2 61.4 reduce-scatter.23
  1052.6 59.7 all-reduce.14
  1115.8 64.1 reduce-scatter.29
  1183.9 62.9 reduce-scatter.27
  1250.9 68.1 reduce-scatter.31
  1323.1 68.1 reduce-scatter.25
  1394.7 178.7 reduce-scatter.37
  1577.4 178.8 reduce-scatter.35
  1759.8 179.0 reduce-scatter.33

commit v2 on v1

v2 whole, which is shorter than its diff:
```python
import math

import jax
import jax.numpy as jnp
from jax import lax
from jax.sharding import PartitionSpec as P

HD = 256
SOFTCAP = 50.0
WIDTHS = (8, 4, 2)
GROUPS = ((0, 1, 2),)
BF = jnp.bfloat16
F32 = jnp.float32


def codes(master, width):
    capped = jnp.minimum(jnp.maximum(master.astype(F32), -128.0), 127.5)
    if width == 0:
        return jnp.floor(capped).astype(BF)
    step = 16.0 if width == 1 else 64.0
    return (jnp.floor(capped * (1.0 / step)) + 0.5).astype(BF)


STEP = (1.0, 16.0, 64.0)


def dot_rows(left, right):
    return lax.dot_general(left, right, (((1,), (1,)), ((), ())), preferred_element_type=F32)


def dot_cols(left, right):
    return lax.dot_general(left, right, (((0,), (0,)), ((), ())), preferred_element_type=F32)


def dot(left, right):
    return lax.dot_general(left, right, (((1,), (0,)), ((), ())), preferred_element_type=F32)


def inverse_rms(value):
    return lax.rsqrt(jnp.mean(value * value, axis=-1, keepdims=True) + 1e-06)


def rms_back(value, inverse, gain, grad):
    scaled = value * inverse
    gain_grad = jnp.sum(grad * scaled, axis=0, keepdims=True)
    weighted = grad * gain
    mean = jnp.mean(weighted * scaled, axis=-1, keepdims=True)
    return inverse * (weighted - scaled * mean), gain_grad


def doc_info(positions, doc_lengths):
    slots = jnp.arange(doc_lengths.shape[0], dtype=jnp.int32)
    ends = jnp.sum(jnp.where(slots[:, None] <= slots[None, :], doc_lengths[:, None], 0), axis=0)
    before = ends[None, :] <= positions[:, None]
    segment = jnp.sum(before.astype(jnp.int32), axis=1)
    offset = jnp.sum(jnp.where(before, doc_lengths[None, :], 0), axis=1)
    return segment, positions - offset


def rotate(value, cosine, sine):
    half = value.shape[-1] // 2
    first, second = value[:, :half], value[:, half:]
    return jnp.concatenate([first * cosine - second * sine, second * cosine + first * sine], axis=1)


def gelu_parts(gate):
    root = math.sqrt(2.0 / math.pi)
    square = gate * gate
    bend = jnp.tanh(root * gate * (1.0 + 0.044715 * square))
    half = 0.5 * (1.0 + bend)
    slope = half + 0.5 * gate * (1.0 - bend * bend) * root * (1.0 + 3.0 * 0.044715 * square)
    return gate * half, slope


def make_body(seq_size):
    line = seq_size // 2
    core_pairs = [(i, i ^ 1) for i in range(4)]
    far_pairs = [(i, i ^ 2) for i in range(4)]
    side_pairs = [(i, i ^ 1) for i in range(seq_size)]

    def core_swap(value):
        return lax.ppermute(value, "head", core_pairs)

    def far_swap(value):
        return lax.ppermute(value, "head", far_pairs)

    def side_swap(value):
        return lax.ppermute(value, "seq", side_pairs)

    def line_shift(value, hops):
        pairs = [(i, i + 2 * hops) for i in range(seq_size) if 0 <= i + 2 * hops < seq_size]
        return lax.ppermute(value, "seq", pairs)

    def line_turn(value, hops):
        return lax.ppermute(value, "seq", [(i, (i + 2 * hops) % seq_size) for i in range(seq_size)])

    def reduce_head(part):
        count, rows, width = part.shape
        half, quarter = rows // 2, rows // 4
        got = core_swap(part[:, half:].astype(BF))
        both = part[:, :half] + got.astype(F32)
        got = far_swap(both[:, quarter:].astype(BF))
        return both[:, :quarter] + got.astype(F32)

    def gather_head(own):
        two = jnp.concatenate([own, far_swap(own)], axis=1)
        return jnp.concatenate([two, core_swap(two)], axis=1)

    def line_scatter(chunks, place):
        def pick(index):
            return lax.dynamic_index_in_dim(chunks, jnp.clip(index, 0, line - 1), 0, keepdims=False)

        up = down = None
        for step in range(1, line):
            ahead, behind = pick(place + line - step), pick(place - line + step)
            up = line_shift((ahead if up is None else ahead + up.astype(F32)).astype(BF), 1)
            down = line_shift((behind if down is None else behind + down.astype(F32)).astype(BF), -1)
        return pick(place) + up.astype(F32) + down.astype(F32)

    def body(
        tokens, cotangent, doc_lengths, pad_mask, gain_one, gain_two, gain_three, gain_four,
        w_query, w_key, w_value, w_out, w_gate, w_up, w_down,
    ):
        rows, width = tokens.shape
        quarter = rows // 4
        heads = w_query.shape[0] // HD
        hidden = w_gate.shape[0]
        head_all, hidden_all = 4 * w_query.shape[0], 4 * hidden
        sm = 1.0 / (64.0 * math.sqrt(width))
        so = 1.0 / (64.0 * math.sqrt(head_all))
        sf = 1.0 / (64.0 * math.sqrt(hidden_all))
        root_scale = 1.0 / math.sqrt(HD)
        h, s = lax.axis_index("head"), lax.axis_index("seq")
        place, side = s // 2, s % 2
        orders = [h, h ^ 2, h ^ 1, h ^ 3]

        def relative(value):
            return jnp.concatenate(
                [lax.dynamic_slice_in_dim(value, o * quarter, quarter, 0) for o in orders], axis=0
            )

        def natural(value):
            parts = []
            for block in range(4):
                bits = h ^ block
                slot = (bits % 2) * 2 + bits // 2
                parts.append(lax.dynamic_slice_in_dim(value, slot * quarter, quarter, 1))
            return jnp.concatenate(parts, axis=1)

        def halves(master):
            parts = master.reshape(line, 2, hidden // seq_size, width)
            return jnp.concatenate(
                [
                    lax.dynamic_index_in_dim(parts, which, 1, keepdims=False).reshape(hidden // 2, width)
                    for which in (side, 1 - side)
                ],
                axis=0,
            )

        x_all = relative(tokens).astype(F32)
        x_own = x_all[:quarter]
        dy_own = lax.dynamic_slice_in_dim(cotangent, h * quarter, quarter, 1)
        within = jnp.concatenate(
            [o * quarter + jnp.arange(quarter, dtype=jnp.int32) for o in orders], axis=0
        )
        position = s * rows + within
        segment, turn = doc_info(position, doc_lengths)
        freq = jnp.exp(jnp.arange(HD // 2, dtype=F32) * (-2.0 * math.log(10000.0) / HD))
        angle = turn.astype(F32)[:, None] * freq[None, :]
        cosine, sine = jnp.cos(angle), jnp.sin(angle)

        inverse_one = inverse_rms(x_all)
        n1 = (x_all * inverse_one * gain_one).astype(BF)
        master_qkv = jnp.concatenate([w_query, w_key, w_value], axis=0)
        gate_rows, up_rows, down_rows = halves(w_gate), halves(w_up), halves(w_down)

        queries, blocks = [], []
        for w in range(3):
            qkv = dot_rows(n1, codes(master_qkv, w)) * (sm * STEP[w])
            queries.append(
                jnp.concatenate(
                    [rotate(qkv[:, j * HD : (j + 1) * HD], cosine, sine) for j in range(heads)], axis=0
                ).astype(BF)
            )
            key = rotate(qkv[:, heads * HD : (heads + 1) * HD], cosine, sine)
            blocks.append(jnp.concatenate([key, qkv[:, (heads + 1) * HD :]], axis=1).astype(BF))
        pad_row = relative(pad_mask).astype(BF)[None, :]
        pad_block = jnp.pad(pad_row, ((0, 15), (0, 2 * HD - rows)))
        packed = jnp.concatenate(blocks + [pad_block], axis=0)
        near = [packed] + [line_shift(packed, hops) for hops in range(1, line)]
        across = [side_swap(block) for block in near]
        pieces, key_position = [], []
        for hops in range(line):
            for which, block in ((side, near[hops]), (1 - side, across[hops])):
                pieces.append(block)
                key_position.append((2 * (place - hops) + which) * rows + within)
        key_position = jnp.concatenate(key_position, axis=0)
        key_valid = jnp.concatenate([b[3 * rows, :rows] for b in pieces], axis=0) > 0.5
        key_segment, _ = doc_info(key_position, doc_lengths)
        allowed = (
            (segment[:, None] == key_segment[None, :])
            & (key_position[None, :] <= position[:, None])
            & (key_position[None, :] >= 0)
            & (key_valid[None, :] | (key_position[None, :] == position[:, None]))
        )
        allowed = jnp.concatenate([allowed] * heads, axis=0)
        n1_all = lax.all_gather(n1, "seq", axis=0, tiled=True)

        keys, values, probs, slopes, contexts, part_attn = [], [], [], [], [], []
        for w in range(3):
            key = jnp.concatenate([b[w * rows : (w + 1) * rows, :HD] for b in pieces], axis=0)
            value = jnp.concatenate([b[w * rows : (w + 1) * rows, HD:] for b in pieces], axis=0)
            bend = jnp.tanh(dot_rows(queries[w], key) * (root_scale / SOFTCAP))
            expo = jnp.where(allowed, jnp.exp(SOFTCAP * bend), 0.0)
            weight = expo / jnp.sum(expo, axis=1, keepdims=True)
            prob = weight.astype(BF)
            slope = (weight * (1.0 - bend * bend) * root_scale).astype(BF)
            context = dot(prob, value).astype(BF)
            context = jnp.concatenate(
                [context[j * rows : (j + 1) * rows] for j in range(heads)], axis=1
            )
            keys.append(key)
            values.append(value)
            probs.append(prob)
            slopes.append(slope)
            contexts.append(context)
            part_attn.append(dot(context, codes(w_out, w)) * (so * STEP[w]))

        def of(items, group):
            return jnp.stack([items[w] for w in group])

        gain_sums = [jnp.zeros((1, width), F32)] * 4
        out_own, middle_grads = [None] * 3, jnp.zeros((quarter, width), F32)
        d_attns = [None] * 3
        left_down, right_down, left_gate, left_up, right_gate = [], [], [], [], []
        for group in GROUPS:
            n = len(group)
            attn = reduce_head(of(part_attn, group))
            inverse_two = inverse_rms(attn)
            middle = x_own + attn * inverse_two * gain_two
            inverse_three = inverse_rms(middle)
            n2_own = (middle * inverse_three * gain_three).astype(BF)
            n2 = gather_head(n2_own)
            hids, slopes_gate, slopes_up, part_ff = [], [], [], []
            for i, w in enumerate(group):
                gate = dot_rows(n2[i], codes(gate_rows, w)) * (sm * STEP[w])
                up = dot_rows(n2[i], codes(up_rows, w)) * (sm * STEP[w])
                act, slope = gelu_parts(gate)
                hid = (act * up).astype(BF)
                hids.append(hid)
                slopes_gate.append((up * slope).astype(BF))
                slopes_up.append(act.astype(BF))
                part_ff.append(dot(hid, codes(down_rows, w)) * (sf * STEP[w]))
            ff = reduce_head(jnp.stack(part_ff))
            inverse_four = inverse_rms(ff)
            dy = of(dy_own, group).astype(F32)
            result = (middle + ff * inverse_four * gain_four).astype(BF)
            d_ff_own, sums = rms_back(
                ff.reshape(n * quarter, width), inverse_four.reshape(n * quarter, 1), gain_four,
                dy.reshape(n * quarter, width),
            )
            gain_sums[3] = gain_sums[3] + sums
            d_ff = gather_head(d_ff_own.astype(BF).reshape(n, quarter, width))
            d_gates, d_ups, part_n2 = [], [], []
            for i, w in enumerate(group):
                d_hid = (dot_rows(d_ff[i], codes(down_rows, w)) * (sf * STEP[w])).astype(BF).astype(F32)
                d_gate = (d_hid * slopes_gate[i].astype(F32)).astype(BF)
                d_up = (d_hid * slopes_up[i].astype(F32)).astype(BF)
                d_gates.append(d_gate)
                d_ups.append(d_up)
                part_n2.append(
                    (dot(d_gate, codes(gate_rows, w)) + dot(d_up, codes(up_rows, w))) * (sm * STEP[w])
                )
            d_n2 = reduce_head(jnp.stack(part_n2)).reshape(n * quarter, width)
            d_norm, sums = rms_back(
                middle.reshape(n * quarter, width), inverse_three.reshape(n * quarter, 1), gain_three, d_n2
            )
            gain_sums[2] = gain_sums[2] + sums
            d_middle = dy.reshape(n * quarter, width) + d_norm
            d_attn_own, sums = rms_back(
                attn.reshape(n * quarter, width), inverse_two.reshape(n * quarter, 1), gain_two, d_middle
            )
            gain_sums[1] = gain_sums[1] + sums
            middle_grads = middle_grads + jnp.sum(d_middle.reshape(n, quarter, width), axis=0)
            d_attn = gather_head(d_attn_own.astype(BF).reshape(n, quarter, width))
            for i, w in enumerate(group):
                out_own[w] = result[i]
                d_attns[w] = d_attn[i]
            half_rows = rows // 2

            def both_sides(value):
                got = side_swap(value[:, :half_rows])
                got = jnp.concatenate([got, core_swap(got)], axis=1)
                return [value.reshape(n * rows, width), got.reshape(n * rows, width)]

            def both_halves(items):
                item = jnp.concatenate(items, axis=0)
                return [item[:, : hidden // 2], side_swap(item[:, hidden // 2 :])]

            right_gate += both_sides(n2)
            left_down += both_halves(hids)
            right_down += both_sides(d_ff)
            left_gate += both_halves(d_gates)
            left_up += both_halves(d_ups)

        activations = natural(gather_head(jnp.stack(out_own)))
        owned = hidden // seq_size

        def weight_grad(left, right, scale):
            total = dot_cols(jnp.concatenate(left, axis=0), jnp.concatenate(right, axis=0)) * scale
            return line_scatter(total.reshape(line, owned, width), place)

        grad_down = weight_grad(left_down, right_down, sf)
        grad_gate = weight_grad(left_gate, right_gate, sm)
        grad_up = weight_grad(left_up, right_gate, sm)

        d_qs, d_blocks = [], []
        for w in range(3):
            d_context = (dot_rows(d_attns[w], codes(w_out, w)) * (so * STEP[w])).astype(BF)
            d_context = jnp.concatenate(
                [d_context[:, j * HD : (j + 1) * HD] for j in range(heads)], axis=0
            )
            d_prob = dot_rows(d_context, values[w])
            delta = jnp.sum(probs[w].astype(F32) * d_prob, axis=1, keepdims=True)
            d_score = (slopes[w].astype(F32) * (d_prob - delta)).astype(BF)
            d_q = dot(d_score, keys[w]).astype(BF).astype(F32)
            d_qs.append(
                jnp.concatenate(
                    [rotate(d_q[j * rows : (j + 1) * rows], cosine, -sine) for j in range(heads)], axis=1
                ).astype(BF)
            )
            d_key = dot_cols(d_score, queries[w])
            d_value = dot_cols(probs[w], d_context)
            d_blocks.append(
                jnp.concatenate([d_key, d_value], axis=1).reshape(line, 2, rows, 2 * HD)
            )
        d_block = jnp.stack(d_blocks, axis=1)
        got = side_swap(d_block[:, :, 1].astype(BF))
        d_block = d_block[:, :, 0] + got.astype(F32)
        d_kv = d_block[0]
        for hops in range(1, line):
            d_kv = d_kv + line_shift(d_block[hops].astype(BF), -hops).astype(F32)
        d_qkv = []
        part_n1 = jnp.zeros((rows, width), F32)
        for w in range(3):
            d_key = d_kv[w, :, :HD].astype(BF).astype(F32)
            d_qkv.append(
                jnp.concatenate(
                    [d_qs[w], rotate(d_key, cosine, -sine).astype(BF), d_kv[w, :, HD:].astype(BF)], axis=1
                )
            )
            part_n1 = part_n1 + dot(d_qkv[w], codes(master_qkv, w)) * (sm * STEP[w])
        d_n1 = reduce_head(part_n1[None])[0]
        d_norm, sums = rms_back(x_own, inverse_one[:quarter], gain_one, d_n1)
        gain_sums[0] = sums
        grad_tokens = natural(gather_head((middle_grads + d_norm).astype(BF)[None]))[0]

        owned_out = w_out.shape[0] // seq_size
        term = dot_cols(jnp.concatenate(contexts, axis=0), jnp.concatenate(d_attns, axis=0)) * so
        term = term.reshape(line, 2, owned_out, width)
        got = side_swap(lax.dynamic_index_in_dim(term, 1 - side, 1, keepdims=False).astype(BF))
        term = lax.dynamic_index_in_dim(term, side, 1, keepdims=False) + got.astype(F32)
        grad_out = line_scatter(term, place)

        d_sum = (d_qkv[0].astype(F32) + d_qkv[1].astype(F32) + d_qkv[2].astype(F32)).astype(BF).T
        cuts = [w_query.shape[0], w_key.shape[0], w_value.shape[0]]
        sent, begin = [], 0
        for cut in cuts:
            sent.append(d_sum[begin : begin + cut].reshape(seq_size, cut // seq_size, rows))
            begin += cut
        sent = jnp.concatenate(sent, axis=1)
        owned_qkv = sent.shape[1]
        sent = sent.reshape(line, 2, owned_qkv, rows)
        other = side_swap(lax.dynamic_index_in_dim(sent, 1 - side, 1, keepdims=False))
        own = lax.dynamic_index_in_dim(sent, side, 1, keepdims=False)
        both = jnp.stack([own, other], axis=1)
        n1_line = n1_all.reshape(line, 2, rows, width)
        total = jnp.zeros((owned_qkv, width), F32)
        for hops in range(line):
            chunk = lax.dynamic_index_in_dim(both, (place + hops) % line, 0, keepdims=False)
            if hops:
                chunk = line_turn(chunk, hops)
            source = lax.dynamic_index_in_dim(n1_line, (place - hops) % line, 0, keepdims=False)
            for slot, which in ((0, side), (1, 1 - side)):
                total = total + dot(chunk[slot], lax.dynamic_index_in_dim(source, which, 0, keepdims=False))
        total = total * sm
        cut_q, cut_k = cuts[0] // seq_size, cuts[1] // seq_size
        grad_query, grad_key, grad_value = (
            total[:cut_q], total[cut_q : cut_q + cut_k], total[cut_q + cut_k :],
        )

        sums = jnp.concatenate(gain_sums, axis=0)
        sums = sums + core_swap(sums)
        sums = sums + far_swap(sums)
        bit = 1
        while bit < seq_size:
            sums = sums + lax.ppermute(sums, "seq", [(i, i ^ bit) for i in range(seq_size)])
            bit *= 2
        share = width // seq_size
        sums = lax.dynamic_slice_in_dim(sums, s * share, share, 1)
        return (
            activations, grad_tokens, grad_query, grad_key, grad_value, grad_out, grad_gate, grad_up,
            grad_down, sums[0], sums[1], sums[2], sums[3],
        )

    return body


def solution(mesh):
    row, rep, vec = P("head", None), P(), P("seq")
    in_specs = (P("seq", None), P(None, "seq", None), rep, vec, rep, rep, rep, rep) + (row,) * 7
    both = P(("head", "seq"), None)
    out_specs = (P(None, "seq", None), P("seq", None)) + (both,) * 7 + (vec,) * 4
    return jax.shard_map(
        make_body(mesh.shape["seq"]), mesh=mesh, in_specs=in_specs, out_specs=out_specs, check_vma=False
    )
```

time: 1950 us -> 961 us (0.49)
  waiting for transfers between devices: 1170 us -> 337 us
  blocking collectives: 257 us -> 0 us
  starting transfers between devices: 2.08 us -> 160 us
  matrix products: 395 us -> 239 us
  local copies, waits for them, and re-layouts: 27.9 us -> 94.3 us
  other arithmetic: 83.3 us -> 105 us
    reduce_scatter x13 -> x0, waiting for transfers between devices: 986 us -> none  [the longest x7 680 us: body(): lax.psum_scatter(for_sending(totals), 'seq', scatter_dimension=0, tiled=T...]
    ppermute x0 -> x70, waiting for transfers between devices: none -> 337 us  [the longest x30 188 us: line_shift(): return lax.ppermute(value, 'seq', pairs)]
    all_gather x6 -> x0, blocking collectives: 197 us -> none  [the longest x3 100 us: body(): value_piece = lax.all_gather(value_b, 'seq', axis=0, tiled=True)]
    psum x4 -> x0, waiting for transfers between devices: 180 us -> none  [the longest x1 61 us: body(): lax.psum((scale_hidden * product(hidden_b, code_down)).astype(jnp.bfloat1...]
    ppermute x0 -> x70, starting transfers between devices: none -> 160 us  [the longest x30 126 us: line_shift(): return lax.ppermute(value, 'seq', pairs)]
    dot_general x81 -> x60, matrix products: 395 us -> 239 us  [the longest x21 111 us: dot_rows(): lax.dot_general(left, right, (((1,), (1,)), ((), ())), preferred_element_...]
    unnamed x2 -> x0, blocking collectives: 60 us -> none
    reduce_sum x16 -> x8, other arithmetic: 35.3 us -> 5.57 us  [the longest x4 4.31 us: rms_back(): gain_grad = jnp.sum(grad * scaled, axis=0, keepdims=True)]
  transfers between devices with their start and end apart: 17 -> 71, of which waited for: 13 -> 32; matrix products, arithmetic and copies ran while one was open for 13% -> 31% of each run, Pallas kernels for 0% -> 0%
where the time goes in v2:
time: 961 us; the launch traced here: 953 us
  waiting for transfers between devices  337 us (35%)
  matrix products  239 us (25%)
  starting transfers between devices  160 us (17%)
  other arithmetic  105 us (11%)
  local copies, waits for them, and re-layouts  94.3 us (10%)
  between operations  17.5 us (2%)
    ppermute x30, waiting for transfers between devices, line_shift(): return lax.ppermute(value, 'seq', pairs)  188 us
    ppermute x30, starting transfers between devices, line_shift(): return lax.ppermute(value, 'seq', pairs)  126 us
    dot_general x21, matrix products, dot_rows(): lax.dot_general(left, right, (((1,), (1,)), ((), ())), preferred_element_...  111 us
    dot_general x29, matrix products, dot(): lax.dot_general(left, right, (((1,), (0,)), ((), ())), preferred_element_...  85.8 us
    ppermute x10, waiting for transfers between devices, far_swap(): return lax.ppermute(value, 'head', far_pairs)  72.7 us
    ppermute x12, waiting for transfers between devices, side_swap(): return lax.ppermute(value, 'seq', side_pairs)  61.5 us
    dot_general x10, matrix products, dot_cols(): lax.dot_general(left, right, (((0,), (0,)), ((), ())), preferred_element_...  42.6 us
    unnamed x366, local copies, waits for them, and re-layouts  31 us
  transfers between devices with their start and end apart: 71, of which 32 were waited for; matrix products, arithmetic and copies ran while one was open for 31% of the time, Pallas kernels for 0%

profile of v2, /device:TPU:0, one launch (start us, length us, event | category | flops | bytes accessed | tf_op | source)
XLA Modules:
  0.0 952.5 jit_solution(3673981764250223682)
XLA Ops:
  53.4 12.5 %collective-permute-done.3 = bf16[592,512]{1,0:T(8,128)(2,1)} collective-permute-done((bf16[592,512]{1,0:T(8,128)(2,1)}, bf16[592,512]{1,0:T(8,128)(2,1)}, u32[]{:S(2)}, u32[]{:S(2)}) %collective-permute-start.3) | collective-permute-done | bytes 606240 | tf_op jit(solution)/shard_map/ppermute | solution.py:92
  66.4 11.0 %collective-permute-done.5 = bf16[592,512]{1,0:T(8,128)(2,1)} collective-permute-done((bf16[592,512]{1,0:T(8,128)(2,1)}, bf16[592,512]{1,0:T(8,128)(2,1)}, u32[]{:S(2)}, u32[]{:S(2)}) %collective-permute-start.5) | collective-permute-done | bytes 606240 | tf_op jit(solution)/shard_map/ppermute | solution.py:92
  124.9 15.3 %collective-permute-done.8 = bf16[3,48,2304]{2,1,0:T(8,128)(2,1)S(1)} collective-permute-done((bf16[3,48,2304]{2,1,0:T(8,128)(2,1)S(1)}, bf16[3,48,2304]{2,1,0:T(8,128)(2,1)S(1)}, u32[]{:S(2)}, u32[]{:S(2)}) %collective-permute-start.8) | collective-permute-done | bytes 663584 | tf_op jit(solution)/shard_map/ppermute | solution.py:85
  143.9 14.6 %collective-permute-done.9 = bf16[3,48,2304]{2,1,0:T(8,128)(2,1)S(1)} collective-permute-done((bf16[3,48,2304]{2,1,0:T(8,128)(2,1)S(1)}, bf16[3,48,2304]{2,1,0:T(8,128)(2,1)S(1)}, u32[]{:S(2)}, u32[]{:S(2)}) %collective-permute-start.9) | collective-permute-done | bytes 663584 | tf_op jit(solution)/shard_map/ppermute | solution.py:85
  158.7 9.3 constant_dynamic-slice_fusion.17
  168.0 12.3 %constant_dynamic-slice_fusion.13 = (bf16[4,1,288,2304]{3,2,1,0:T(8,128)(2,1)}, bf16[4,1,288,2304]{3,2,1,0:T(8,128)(2,1)}, bf16[4,1,288,2304]{3,2,1,0:T(8,128)(2,1)S(1)}, bf16[4,1,288,2304]{3,2,1,0:T(8,128)(2,1)S(1)}) fusion(bf16[4,2,288,2304]{3,2,1,0:T(8,128)(2,1)} %bitcast.373, s32[]{:T(128)S(6)} %select_n.239, s32[]{:T(128)S(6)} %select_n.240, ...), kind=kLoop, calls=%fused_computation.672 | loop fusion | bytes 42467336 | tf_op jit(solution)/shard_map/jit(dynamic_index_in_dim)/dynamic_slice | solution.py:154
  201.7 9.4 fusion.13
  216.7 11.6 %multiply_convert_fusion.16 = (bf16[192,2304]{1,0:T(8,128)(2,1)}, f32[192,2304]{1,0:T(8,128)}) fusion(f32[192,2304]{1,0:T(8,128)} %fusion.7, bf16[1152,2304]{1,0:T(8,128)(2,1)S(1)} %bitcast.384, bf16[1152,2304]{1,0:T(8,128)(2,1)S(1)} %bitcast.392, bf16[3,192,2304]{2,1,0:T(8,128)(2,1)S(1)} %pad_maximum_fusion.14), kind=kOutput, calls=%fused_computation.215 | convolution fusion | flops 2091515904 | bytes 15925248 | tf_op jit(solution)/shard_map/dot_general | solution.py:28
  242.1 11.3 %multiply_convert_fusion.15 = (bf16[192,2304]{1,0:T(8,128)(2,1)}, f32[192,2304]{1,0:T(8,128)}) fusion(f32[192,2304]{1,0:T(8,128)} %fusion.13, bf16[1152,2304]{1,0:T(8,128)(2,1)S(1)} %bitcast.385, bf16[1152,2304]{1,0:T(8,128)(2,1)S(1)} %bitcast.393, bf16[3,192,2304]{2,1,0:T(8,128)(2,1)S(1)} %pad_maximum_fusion.14), kind=kOutput, calls=%fused_computation.211 | convolution fusion | flops 2091515904 | bytes 15925248 | tf_op jit(solution)/shard_map/dot_general | solution.py:28
  253.4 8.0 fusion.45
  267.6 14.9 %collective-permute-done.12 = bf16[3,48,2304]{2,1,0:T(8,128)(2,1)S(1)} collective-permute-done((bf16[3,48,2304]{2,1,0:T(8,128)(2,1)S(1)}, bf16[3,48,2304]{2,1,0:T(8,128)(2,1)S(1)}, u32[]{:S(2)}, u32[]{:S(2)}) %collective-permute-start.12) | collective-permute-done | bytes 663584 | tf_op jit(solution)/shard_map/ppermute | solution.py:85
  286.2 11.9 %collective-permute-done.41 = bf16[3,96,2304]{2,1,0:T(8,128)(2,1)} collective-permute-done((bf16[3,96,2304]{2,1,0:T(8,128)(2,1)S(1)}, bf16[3,96,2304]{2,1,0:T(8,128)(2,1)}, u32[]{:S(2)}, u32[]{:S(2)}) %collective-permute-start.41) | collective-permute-done | bytes 1327136 | tf_op jit(solution)/shard_map/ppermute | solution.py:88
  309.4 7.9 collective-permute-done.13
  320.2 11.2 %multiply_convert_fusion.12 = (bf16[192,2304]{1,0:T(8,128)(2,1)}, bf16[192,2304]{1,0:T(8,128)(2,1)S(1)}) fusion(f32[192,2304]{1,0:T(8,128)} %copy-done.162, f32[192,2304]{1,0:T(8,128)} %get-tuple-element.224, bf16[1152,2304]{1,0:T(8,128)(2,1)S(1)} %bitcast.415, bf16[1152,2304]{1,0:T(8,128)(2,1)S(1)} %bitcast.407, bf16[3,192,2304]{2,1,0:T(8,128)(2,1)} %pad_maximum_fusion.17), kind=kOutput, calls=%fused_computation.208 | convolution fusion | flops 2088861696 | bytes 16809984 | tf_op jit(solution)/shard_map/dot_general | solution.py:28
  338.8 12.0 %multiply_convert_fusion.9 = (bf16[192,2304]{1,0:T(8,128)(2,1)}, bf16[192,2304]{1,0:T(8,128)(2,1)S(1)}) fusion(f32[192,2304]{1,0:T(8,128)} %fusion.7, f32[192,2304]{1,0:T(8,128)} %get-tuple-element.222, bf16[1152,2304]{1,0:T(8,128)(2,1)S(1)} %bitcast.416, bf16[1152,2304]{1,0:T(8,128)(2,1)S(1)} %bitcast.408, bf16[3,192,2304]{2,1,0:T(8,128)(2,1)S(1)} %copy-done.40), kind=kOutput, calls=%fused_computation.205 | convolution fusion | flops 2099478528 | bytes 16809984 | tf_op jit(solution)/shard_map/dot_general | solution.py:28
  350.8 9.4 fusion.6
  360.2 13.8 %multiply_convert_fusion.6 = (bf16[192,2304]{1,0:T(8,128)(2,1)}, bf16[192,2304]{1,0:T(8,128)(2,1)S(1)}) fusion(f32[192,2304]{1,0:T(8,128)} %fusion.13, f32[192,2304]{1,0:T(8,128)} %get-tuple-element.220, bf16[1152,2304]{1,0:T(8,128)(2,1)} %bitcast.412, bf16[1152,2304]{1,0:T(8,128)(2,1)} %bitcast.399, bf16[3,192,2304]{2,1,0:T(8,128)(2,1)S(1)} %copy-done.40), kind=kOutput, calls=%fused_computation.202 | convolution fusion | flops 2099478528 | bytes 16809984 | tf_op jit(solution)/shard_map/dot_general | solution.py:28
  374.0 7.8 fusion.12
  412.1 8.7 convolution_multiply_fusion
  422.6 32.8 %collective-permute-start.59 = (bf16[288,2304]{1,0:T(8,128)(2,1)}, bf16[288,2304]{1,0:T(8,128)(2,1)}, u32[]{:S(2)}, u32[]{:S(2)}) collective-permute-start(bf16[288,2304]{1,0:T(8,128)(2,1)} %get-tuple-element.46), channel_id=1, source_target_pairs={{0,2},{1,3},{2,4},{3,5},{4,6},{5,7},{8,10},{9,11},{10,12},{11,13},... | collective-permute-start | bytes 3981320 | tf_op jit(solution)/shard_map/ppermute | solution.py:92
  458.0 9.5 convolution_multiply_fusion.1
  469.2 8.8 collective-permute-start.50
  479.3 12.1 %convolution_multiply_fusion.2 = f32[1152,2304]{1,0:T(8,128)} fusion(bf16[576,2304]{1,0:T(8,128)(2,1)} %bitcast.436, bf16[576,2304]{1,0:T(8,128)(2,1)S(1)} %bitcast.434, bf16[576,1152]{1,0:T(8,128)(2,1)} %collective-permute-done.40, bf16[576,1152]{1,0:T(8,128)(2,1)S(1)} %copy-done.53), kind=kOutput, calls=%fused_computation.14 | convolution fusion | flops 6133874688 | bytes 18579456 | tf_op jit(solution)/shard_map/dot_general | solution.py:32
  495.5 15.8 %collective-permute-start.43 = (bf16[288,2304]{1,0:T(8,128)(2,1)S(1)}, bf16[288,2304]{1,0:T(8,128)(2,1)S(1)}, u32[]{:S(2)}, u32[]{:S(2)}) collective-permute-start(bf16[288,2304]{1,0:T(8,128)(2,1)S(1)} %get-tuple-element.54), channel_id=1, source_target_pairs={{0,2},{1,3},{2,4},{3,5},{4,6},{5,7},{8,10},{9,11},{10,12},{11,13},... | collective-permute-start | bytes 3981320 | tf_op jit(solution)/shard_map/ppermute | solution.py:92
  519.9 12.4 %collective-permute-done.19 = bf16[3,48,2304]{2,1,0:T(8,128)(2,1)S(1)} collective-permute-done((bf16[3,48,2304]{2,1,0:T(8,128)(2,1)S(1)}, bf16[3,48,2304]{2,1,0:T(8,128)(2,1)S(1)}, u32[]{:S(2)}, u32[]{:S(2)}) %collective-permute-start.19) | collective-permute-done | bytes 663584 | tf_op jit(solution)/shard_map/ppermute | solution.py:85
  626.8 9.6 %collective-permute-done.44 = bf16[288,2304]{1,0:T(8,128)(2,1)} collective-permute-done((bf16[288,2304]{1,0:T(8,128)(2,1)S(1)}, bf16[288,2304]{1,0:T(8,128)(2,1)}, u32[]{:S(2)}, u32[]{:S(2)}) %collective-permute-start.44) | collective-permute-done | bytes 1327136 | tf_op jit(solution)/shard_map/ppermute | solution.py:92
  643.3 42.1 %collective-permute-done.33 = bf16[4,64,2304]{2,1,0:T(8,128)(2,1)} collective-permute-done((bf16[4,64,2304]{2,1,0:T(8,128)(2,1)}, bf16[4,64,2304]{2,1,0:T(8,128)(2,1)}, u32[]{:S(2)}, u32[]{:S(2)}) %collective-permute-start.33) | collective-permute-done | bytes 1179680 | tf_op jit(solution)/shard_map/ppermute | solution.py:88
  711.9 28.6 %collective-permute-done.38 = bf16[64,2304]{1,0:T(8,128)(2,1)S(1)} collective-permute-done((bf16[64,2304]{1,0:T(8,128)(2,1)S(1)}, bf16[64,2304]{1,0:T(8,128)(2,1)S(1)}, u32[]{:S(2)}, u32[]{:S(2)}) %collective-permute-start.38) | collective-permute-done | bytes 294944 | tf_op jit(solution)/shard_map/ppermute | solution.py:92
  763.2 27.0 %collective-permute-done.64 = bf16[288,2304]{1,0:T(8,128)(2,1)S(1)} collective-permute-done((bf16[288,2304]{1,0:T(8,128)(2,1)S(1)}, bf16[288,2304]{1,0:T(8,128)(2,1)S(1)}, u32[]{:S(2)}, u32[]{:S(2)}) %collective-permute-start.64) | collective-permute-done | bytes 1327136 | tf_op jit(solution)/shard_map/ppermute | solution.py:92
  796.6 22.0 %collective-permute-done.55 = bf16[288,2304]{1,0:T(8,128)(2,1)S(1)} collective-permute-done((bf16[288,2304]{1,0:T(8,128)(2,1)}, bf16[288,2304]{1,0:T(8,128)(2,1)S(1)}, u32[]{:S(2)}, u32[]{:S(2)}) %collective-permute-start.55) | collective-permute-done | bytes 1327136 | tf_op jit(solution)/shard_map/ppermute | solution.py:92
  823.7 22.0 %collective-permute-done.48 = bf16[288,2304]{1,0:T(8,128)(2,1)S(1)} collective-permute-done((bf16[288,2304]{1,0:T(8,128)(2,1)S(1)}, bf16[288,2304]{1,0:T(8,128)(2,1)S(1)}, u32[]{:S(2)}, u32[]{:S(2)}) %collective-permute-start.48) | collective-permute-done | bytes 1327136 | tf_op jit(solution)/shard_map/ppermute | solution.py:92
  856.3 31.8 %collective-permute-done.23 = bf16[3,192,512]{2,1,0:T(8,128)(2,1)S(1)} collective-permute-done((bf16[3,192,512]{2,1,0:T(8,128)(2,1)S(1)}, bf16[3,192,512]{2,1,0:T(8,128)(2,1)S(1)}, u32[]{:S(2)}, u32[]{:S(2)}) %collective-permute-start.23) | collective-permute-done | bytes 589856 | tf_op jit(solution)/shard_map/ppermute | solution.py:92
  (720 shorter events, 447.6 us)
Async XLA Ops:
  7.2 900.6 %all-gather.2.cloned.1.call-start = ((), (), s32[]{:S(2)}) async-start(), calls=%async_computation | async-start | bytes 7962624 | tf_op jit(solution)/shard_map/all_gather | solution.py:207
  32.0 45.9 %collective-permute-start = (bf16[592,512]{1,0:T(8,128)(2,1)}, bf16[592,512]{1,0:T(8,128)(2,1)}, u32[]{:S(2)}, u32[]{:S(2)}) collective-permute-start(bf16[592,512]{1,0:T(8,128)(2,1)} %pad_maximum_fusion.29), channel_id=1, source_target_pairs={{0,1},{1,0},{2,3},{3,2},{4,5},{5,4},{6,7},{7,6},{8,9},{9,8},{10,11... | collective-permute-start | bytes 1818632 | tf_op jit(solution)/shard_map/ppermute | solution.py:88
  43.8 33.6 %collective-permute-start.5 = (bf16[592,512]{1,0:T(8,128)(2,1)}, bf16[592,512]{1,0:T(8,128)(2,1)}, u32[]{:S(2)}, u32[]{:S(2)}) collective-permute-start(bf16[592,512]{1,0:T(8,128)(2,1)} %pad_maximum_fusion.29), channel_id=1, source_target_pairs={{0,6},{1,7},{8,14},{9,15},{16,22},{17,23},{24,30},{25,31}} | collective-permute-start | bytes 1818632 | tf_op jit(solution)/shard_map/ppermute | solution.py:92
  52.9 40.7 %collective-permute-start.2 = (bf16[592,512]{1,0:T(8,128)(2,1)}, bf16[592,512]{1,0:T(8,128)(2,1)S(1)}, u32[]{:S(2)}, u32[]{:S(2)}) collective-permute-start(bf16[592,512]{1,0:T(8,128)(2,1)} %collective-permute-done.1), channel_id=1, source_target_pairs={{0,1},{1,0},{2,3},{3,2},{4,5},{5,4},{6,7},{7,6},{8,9},{9,8},{10,11... | collective-permute-start | bytes 1818632 | tf_op jit(solution)/shard_map/ppermute | solution.py:88
  303.7 108.4 %collective-permute-start.56 = (bf16[576,1152]{1,0:T(8,128)(2,1)}, bf16[576,1152]{1,0:T(8,128)(2,1)}, u32[]{:S(2)}, u32[]{:S(2)}) collective-permute-start(bf16[576,1152]{1,0:T(8,128)(2,1)} %get-tuple-element.71), channel_id=1, source_target_pairs={{0,1},{1,0},{2,3},{3,2},{4,5},{5,4},{6,7},{7,6},{8,9},{9,8},{10,11... | collective-permute-start | bytes 3981320 | tf_op jit(solution)/shard_map/ppermute | solution.py:88
  308.1 95.8 %collective-permute-start.57 = (bf16[3,96,2304]{2,1,0:T(8,128)(2,1)}, bf16[3,96,2304]{2,1,0:T(8,128)(2,1)}, u32[]{:S(2)}, u32[]{:S(2)}) collective-permute-start(bf16[3,96,2304]{2,1,0:T(8,128)(2,1)} %pad_maximum_fusion.26), channel_id=1, source_target_pairs={{0,1},{1,0},{2,3},{3,2},{4,5},{5,4},{6,7},{7,6},{8,9},{9,8},{10,11... | collective-permute-start | bytes 3981320 | tf_op jit(solution)/shard_map/ppermute | solution.py:88
  318.5 86.5 %collective-permute-start.14 = (bf16[3,96,2304]{2,1,0:T(8,128)(2,1)}, bf16[3,96,2304]{2,1,0:T(8,128)(2,1)}, u32[]{:S(2)}, u32[]{:S(2)}) collective-permute-start(bf16[3,96,2304]{2,1,0:T(8,128)(2,1)} %pad_maximum_fusion.25), channel_id=1, source_target_pairs={{0,8},{8,0},{16,24},{24,16},{1,9},{9,1},{17,25},{25,17},{2,10},{10... | collective-permute-start | bytes 3981320 | tf_op jit(solution)/shard_map/ppermute | solution.py:82
  401.0 55.9 %collective-permute-start.49 = (bf16[576,1152]{1,0:T(8,128)(2,1)S(1)}, bf16[576,1152]{1,0:T(8,128)(2,1)S(1)}, u32[]{:S(2)}, u32[]{:S(2)}) collective-permute-start(bf16[576,1152]{1,0:T(8,128)(2,1)S(1)} %get-tuple-element.73), channel_id=1, source_target_pairs={{0,1},{1,0},{2,3},{3,2},{4,5},{5,4},{6,7},{7,6},{8,9},{9,8},{10,11... | collective-permute-start | bytes 3981320 | tf_op jit(solution)/shard_map/ppermute | solution.py:88
  403.9 74.2 %collective-permute-start.40 = (bf16[576,1152]{1,0:T(8,128)(2,1)}, bf16[576,1152]{1,0:T(8,128)(2,1)}, u32[]{:S(2)}, u32[]{:S(2)}) collective-permute-start(bf16[576,1152]{1,0:T(8,128)(2,1)} %get-tuple-element.75), channel_id=1, source_target_pairs={{0,1},{1,0},{2,3},{3,2},{4,5},{5,4},{6,7},{7,6},{8,9},{9,8},{10,11... | collective-permute-start | bytes 3981320 | tf_op jit(solution)/shard_map/ppermute | solution.py:88
  409.6 85.8 %collective-permute-start.18 = (bf16[3,48,2304]{2,1,0:T(8,128)(2,1)}, bf16[3,48,2304]{2,1,0:T(8,128)(2,1)S(1)}, u32[]{:S(2)}, u32[]{:S(2)}) collective-permute-start(bf16[3,48,2304]{2,1,0:T(8,128)(2,1)} %slice.1227), channel_id=1, source_target_pairs={{0,16},{8,24},{16,0},{24,8},{1,17},{9,25},{17,1},{25,9},{2,18},{10... | collective-permute-start | bytes 1990664 | tf_op jit(solution)/shard_map/ppermute | solution.py:85
  422.6 93.9 %collective-permute-start.59 = (bf16[288,2304]{1,0:T(8,128)(2,1)}, bf16[288,2304]{1,0:T(8,128)(2,1)}, u32[]{:S(2)}, u32[]{:S(2)}) collective-permute-start(bf16[288,2304]{1,0:T(8,128)(2,1)} %get-tuple-element.46), channel_id=1, source_target_pairs={{0,2},{1,3},{2,4},{3,5},{4,6},{5,7},{8,10},{9,11},{10,12},{11,13},... | collective-permute-start | bytes 3981320 | tf_op jit(solution)/shard_map/ppermute | solution.py:92
  455.4 148.0 %collective-permute-start.62 = (bf16[288,2304]{1,0:T(8,128)(2,1)}, bf16[288,2304]{1,0:T(8,128)(2,1)}, u32[]{:S(2)}, u32[]{:S(2)}) collective-permute-start(bf16[288,2304]{1,0:T(8,128)(2,1)} %get-tuple-element.47), channel_id=1, source_target_pairs={{2,0},{3,1},{4,2},{5,3},{6,4},{7,5},{10,8},{11,9},{12,10},{13,11},... | collective-permute-start | bytes 3981320 | tf_op jit(solution)/shard_map/ppermute | solution.py:92
  469.2 64.5 %collective-permute-start.50 = (bf16[288,2304]{1,0:T(8,128)(2,1)}, bf16[288,2304]{1,0:T(8,128)(2,1)}, u32[]{:S(2)}, u32[]{:S(2)}) collective-permute-start(bf16[288,2304]{1,0:T(8,128)(2,1)} %get-tuple-element.50), channel_id=1, source_target_pairs={{0,2},{1,3},{2,4},{3,5},{4,6},{5,7},{8,10},{9,11},{10,12},{11,13},... | collective-permute-start | bytes 3981320 | tf_op jit(solution)/shard_map/ppermute | solution.py:92
  478.0 135.2 %collective-permute-start.53 = (bf16[288,2304]{1,0:T(8,128)(2,1)}, bf16[288,2304]{1,0:T(8,128)(2,1)}, u32[]{:S(2)}, u32[]{:S(2)}) collective-permute-start(bf16[288,2304]{1,0:T(8,128)(2,1)} %get-tuple-element.51), channel_id=1, source_target_pairs={{2,0},{3,1},{4,2},{5,3},{6,4},{7,5},{10,8},{11,9},{12,10},{13,11},... | collective-permute-start | bytes 3981320 | tf_op jit(solution)/shard_map/ppermute | solution.py:92
  495.5 44.8 %collective-permute-start.43 = (bf16[288,2304]{1,0:T(8,128)(2,1)S(1)}, bf16[288,2304]{1,0:T(8,128)(2,1)S(1)}, u32[]{:S(2)}, u32[]{:S(2)}) collective-permute-start(bf16[288,2304]{1,0:T(8,128)(2,1)S(1)} %get-tuple-element.54), channel_id=1, source_target_pairs={{0,2},{1,3},{2,4},{3,5},{4,6},{5,7},{8,10},{9,11},{10,12},{11,13},... | collective-permute-start | bytes 3981320 | tf_op jit(solution)/shard_map/ppermute | solution.py:92
  532.3 89.9 %collective-permute-start.46 = (bf16[288,2304]{1,0:T(8,128)(2,1)}, bf16[288,2304]{1,0:T(8,128)(2,1)}, u32[]{:S(2)}, u32[]{:S(2)}) collective-permute-start(bf16[288,2304]{1,0:T(8,128)(2,1)} %get-tuple-element.55), channel_id=1, source_target_pairs={{2,0},{3,1},{4,2},{5,3},{6,4},{7,5},{10,8},{11,9},{12,10},{13,11},... | collective-permute-start | bytes 3981320 | tf_op jit(solution)/shard_map/ppermute | solution.py:92
  540.2 67.8 %collective-permute-start.60 = (bf16[288,2304]{1,0:T(8,128)(2,1)}, bf16[288,2304]{1,0:T(8,128)(2,1)}, u32[]{:S(2)}, u32[]{:S(2)}) collective-permute-start(bf16[288,2304]{1,0:T(8,128)(2,1)} %fusion.81), channel_id=1, source_target_pairs={{0,2},{1,3},{2,4},{3,5},{4,6},{5,7},{8,10},{9,11},{10,12},{11,13},... | collective-permute-start | bytes 3981320 | tf_op jit(solution)/shard_map/ppermute | solution.py:92
  548.8 65.8 %collective-permute-start.51 = (bf16[288,2304]{1,0:T(8,128)(2,1)}, bf16[288,2304]{1,0:T(8,128)(2,1)}, u32[]{:S(2)}, u32[]{:S(2)}) collective-permute-start(bf16[288,2304]{1,0:T(8,128)(2,1)} %fusion.86), channel_id=1, source_target_pairs={{0,2},{1,3},{2,4},{3,5},{4,6},{5,7},{8,10},{9,11},{10,12},{11,13},... | collective-permute-start | bytes 3981320 | tf_op jit(solution)/shard_map/ppermute | solution.py:92
  608.0 150.3 %collective-permute-start.21 = (bf16[4,3,192,512]{3,2,1,0:T(8,128)(2,1)}, bf16[4,3,192,512]{3,2,1,0:T(8,128)(2,1)S(1)}, u32[]{:S(2)}, u32[]{:S(2)}) collective-permute-start(bf16[4,3,192,512]{3,2,1,0:T(8,128)(2,1)} %fusion.96), channel_id=1, source_target_pairs={{0,1},{1,0},{2,3},{3,2},{4,5},{5,4},{6,7},{7,6},{8,9},{9,8},{10,11... | collective-permute-start | bytes 7077896 | tf_op jit(solution)/shard_map/ppermute | solution.py:88
  613.3 80.8 %collective-permute-start.63 = (bf16[288,2304]{1,0:T(8,128)(2,1)}, bf16[288,2304]{1,0:T(8,128)(2,1)}, u32[]{:S(2)}, u32[]{:S(2)}) collective-permute-start(bf16[288,2304]{1,0:T(8,128)(2,1)} %get-tuple-element.45), channel_id=1, source_target_pairs={{2,0},{3,1},{4,2},{5,3},{6,4},{7,5},{10,8},{11,9},{12,10},{13,11},... | collective-permute-start | bytes 3981320 | tf_op jit(solution)/shard_map/ppermute | solution.py:92
  614.6 70.8 %collective-permute-start.33 = (bf16[4,64,2304]{2,1,0:T(8,128)(2,1)}, bf16[4,64,2304]{2,1,0:T(8,128)(2,1)}, u32[]{:S(2)}, u32[]{:S(2)}) collective-permute-start(bf16[4,64,2304]{2,1,0:T(8,128)(2,1)} %fusion.130), channel_id=1, source_target_pairs={{0,1},{1,0},{2,3},{3,2},{4,5},{5,4},{6,7},{7,6},{8,9},{9,8},{10,11... | collective-permute-start | bytes 3538952 | tf_op jit(solution)/shard_map/ppermute | solution.py:88
  622.2 138.5 %collective-permute-start.61 = (bf16[288,2304]{1,0:T(8,128)(2,1)}, bf16[288,2304]{1,0:T(8,128)(2,1)S(1)}, u32[]{:S(2)}, u32[]{:S(2)}) collective-permute-start(bf16[288,2304]{1,0:T(8,128)(2,1)} %get-tuple-element.44), channel_id=1, source_target_pairs={{0,2},{1,3},{2,4},{3,5},{4,6},{5,7},{8,10},{9,11},{10,12},{11,13},... | collective-permute-start | bytes 3981320 | tf_op jit(solution)/shard_map/ppermute | solution.py:92
  636.5 70.7 %collective-permute-start.54 = (bf16[288,2304]{1,0:T(8,128)(2,1)}, bf16[288,2304]{1,0:T(8,128)(2,1)}, u32[]{:S(2)}, u32[]{:S(2)}) collective-permute-start(bf16[288,2304]{1,0:T(8,128)(2,1)} %get-tuple-element.49), channel_id=1, source_target_pairs={{2,0},{3,1},{4,2},{5,3},{6,4},{7,5},{10,8},{11,9},{12,10},{13,11},... | collective-permute-start | bytes 3981320 | tf_op jit(solution)/shard_map/ppermute | solution.py:92
  701.7 93.6 %collective-permute-start.52 = (bf16[288,2304]{1,0:T(8,128)(2,1)}, bf16[288,2304]{1,0:T(8,128)(2,1)S(1)}, u32[]{:S(2)}, u32[]{:S(2)}) collective-permute-start(bf16[288,2304]{1,0:T(8,128)(2,1)} %get-tuple-element.48), channel_id=1, source_target_pairs={{0,2},{1,3},{2,4},{3,5},{4,6},{5,7},{8,10},{9,11},{10,12},{11,13},... | collective-permute-start | bytes 3981320 | tf_op jit(solution)/shard_map/ppermute | solution.py:92
  705.7 37.5 %collective-permute-start.47 = (bf16[288,2304]{1,0:T(8,128)(2,1)S(1)}, bf16[288,2304]{1,0:T(8,128)(2,1)S(1)}, u32[]{:S(2)}, u32[]{:S(2)}) collective-permute-start(bf16[288,2304]{1,0:T(8,128)(2,1)S(1)} %copy-done.56), channel_id=1, source_target_pairs={{2,0},{3,1},{4,2},{5,3},{6,4},{7,5},{10,8},{11,9},{12,10},{13,11},... | collective-permute-start | bytes 3981320 | tf_op jit(solution)/shard_map/ppermute | solution.py:92
  749.8 73.9 %collective-permute-start.45 = (bf16[288,2304]{1,0:T(8,128)(2,1)}, bf16[288,2304]{1,0:T(8,128)(2,1)S(1)}, u32[]{:S(2)}, u32[]{:S(2)}) collective-permute-start(bf16[288,2304]{1,0:T(8,128)(2,1)} %get-tuple-element.52), channel_id=1, source_target_pairs={{0,2},{1,3},{2,4},{3,5},{4,6},{5,7},{8,10},{9,11},{10,12},{11,13},... | collective-permute-start | bytes 3981320 | tf_op jit(solution)/shard_map/ppermute | solution.py:92
  756.1 34.0 %collective-permute-start.64 = (bf16[288,2304]{1,0:T(8,128)(2,1)S(1)}, bf16[288,2304]{1,0:T(8,128)(2,1)S(1)}, u32[]{:S(2)}, u32[]{:S(2)}) collective-permute-start(bf16[288,2304]{1,0:T(8,128)(2,1)S(1)} %fusion.80), channel_id=1, source_target_pairs={{2,0},{3,1},{4,2},{5,3},{6,4},{7,5},{10,8},{11,9},{12,10},{13,11},... | collective-permute-start | bytes 3981320 | tf_op jit(solution)/shard_map/ppermute | solution.py:92
  758.3 60.3 %collective-permute-start.55 = (bf16[288,2304]{1,0:T(8,128)(2,1)}, bf16[288,2304]{1,0:T(8,128)(2,1)S(1)}, u32[]{:S(2)}, u32[]{:S(2)}) collective-permute-start(bf16[288,2304]{1,0:T(8,128)(2,1)} %fusion.85), channel_id=1, source_target_pairs={{2,0},{3,1},{4,2},{5,3},{6,4},{7,5},{10,8},{11,9},{12,10},{13,11},... | collective-permute-start | bytes 3981320 | tf_op jit(solution)/shard_map/ppermute | solution.py:92
  761.9 83.8 %collective-permute-start.48 = (bf16[288,2304]{1,0:T(8,128)(2,1)S(1)}, bf16[288,2304]{1,0:T(8,128)(2,1)S(1)}, u32[]{:S(2)}, u32[]{:S(2)}) collective-permute-start(bf16[288,2304]{1,0:T(8,128)(2,1)S(1)} %copy-done.55), channel_id=1, source_target_pairs={{2,0},{3,1},{4,2},{5,3},{6,4},{7,5},{10,8},{11,9},{12,10},{13,11},... | collective-permute-start | bytes 3981320 | tf_op jit(solution)/shard_map/ppermute | solution.py:92
  790.2 66.2 %collective-permute-start.22 = (bf16[3,192,512]{2,1,0:T(8,128)(2,1)S(1)}, bf16[3,192,512]{2,1,0:T(8,128)(2,1)S(1)}, u32[]{:S(2)}, u32[]{:S(2)}) collective-permute-start(bf16[3,192,512]{2,1,0:T(8,128)(2,1)S(1)} %get-tuple-element.87), channel_id=1, source_target_pairs={{2,0},{3,1},{4,2},{5,3},{6,4},{7,5},{10,8},{11,9},{12,10},{13,11},... | collective-permute-start | bytes 1769480 | tf_op jit(solution)/shard_map/ppermute | solution.py:92
  795.3 92.9 %collective-permute-start.23 = (bf16[3,192,512]{2,1,0:T(8,128)(2,1)S(1)}, bf16[3,192,512]{2,1,0:T(8,128)(2,1)S(1)}, u32[]{:S(2)}, u32[]{:S(2)}) collective-permute-start(bf16[3,192,512]{2,1,0:T(8,128)(2,1)S(1)} %get-tuple-element.89), channel_id=1, source_target_pairs={{4,0},{5,1},{6,2},{7,3},{12,8},{13,9},{14,10},{15,11},{20,16},{21,... | collective-permute-start | bytes 1769480 | tf_op jit(solution)/shard_map/ppermute | solution.py:92
  818.6 69.6 %collective-permute-start.24 = (bf16[3,192,512]{2,1,0:T(8,128)(2,1)S(1)}, bf16[3,192,512]{2,1,0:T(8,128)(2,1)S(1)}, u32[]{:S(2)}, u32[]{:S(2)}) collective-permute-start(bf16[3,192,512]{2,1,0:T(8,128)(2,1)S(1)} %get-tuple-element.88), channel_id=1, source_target_pairs={{6,0},{7,1},{14,8},{15,9},{22,16},{23,17},{30,24},{31,25}} | collective-permute-start | bytes 1769480 | tf_op jit(solution)/shard_map/ppermute | solution.py:92
  (218 other events, 2553.5 us)
Sparse Core Ops, SparseCore 0:
  285.7 165.9 all-gather.1

commit v3 on v2

v3 whole, which is shorter than its diff:
```python
import functools
import math

import jax
import jax.numpy as jnp
from jax import lax
from jax.experimental import pallas as pl
from jax.experimental.pallas import tpu as pltpu
from jax.sharding import PartitionSpec as P

HD = 256
SOFTCAP = 50.0
WIDTHS = (8, 4, 2)
BF = jnp.bfloat16
F32 = jnp.float32


def codes(master, width):
    capped = jnp.minimum(jnp.maximum(master.astype(F32), -128.0), 127.5)
    if width == 0:
        return jnp.floor(capped).astype(BF)
    step = 16.0 if width == 1 else 64.0
    return (jnp.floor(capped * (1.0 / step)) + 0.5).astype(BF)


STEP = (1.0, 16.0, 64.0)


def dot_rows(left, right):
    return lax.dot_general(left, right, (((1,), (1,)), ((), ())), preferred_element_type=F32)


def dot_cols(left, right):
    return lax.dot_general(left, right, (((0,), (0,)), ((), ())), preferred_element_type=F32)


def dot(left, right):
    return lax.dot_general(left, right, (((1,), (0,)), ((), ())), preferred_element_type=F32)


def inverse_rms(value):
    return lax.rsqrt(jnp.mean(value * value, axis=-1, keepdims=True) + 1e-06)


def rms_back(value, inverse, gain, grad):
    scaled = value * inverse
    gain_grad = jnp.sum(grad * scaled, axis=0, keepdims=True)
    weighted = grad * gain
    mean = jnp.mean(weighted * scaled, axis=-1, keepdims=True)
    return inverse * (weighted - scaled * mean), gain_grad


def doc_info(positions, doc_lengths):
    slots = jnp.arange(doc_lengths.shape[0], dtype=jnp.int32)
    ends = jnp.sum(jnp.where(slots[:, None] <= slots[None, :], doc_lengths[:, None], 0), axis=0)
    before = ends[None, :] <= positions[:, None]
    segment = jnp.sum(before.astype(jnp.int32), axis=1)
    offset = jnp.sum(jnp.where(before, doc_lengths[None, :], 0), axis=1)
    return segment, positions - offset


def rotate(value, cosine, sine):
    half = value.shape[-1] // 2
    first, second = value[:, :half], value[:, half:]
    return jnp.concatenate([first * cosine - second * sine, second * cosine + first * sine], axis=1)


def gelu_parts(gate):
    root = math.sqrt(2.0 / math.pi)
    square = gate * gate
    bend = jnp.tanh(root * gate * (1.0 + 0.044715 * square))
    half = 0.5 * (1.0 + bend)
    slope = half + 0.5 * gate * (1.0 - bend * bend) * root * (1.0 + 3.0 * 0.044715 * square)
    return gate * half, slope


def all_codes(master):
    capped = jnp.minimum(jnp.maximum(master.astype(F32), -128.0), 127.5)
    return [
        jnp.floor(capped).astype(BF),
        (jnp.floor(capped * (1.0 / STEP[1])) + 0.5).astype(BF),
        (jnp.floor(capped * (1.0 / STEP[2])) + 0.5).astype(BF),
    ]


PARTS = 3
VMEM = 60 * 2**20


def hidden_call(kernel, side, acts, tiles, weights, out_count, cost):
    line, _, owned, width = weights[0].shape
    rows = acts[0].shape[1]
    piece = owned // PARTS
    block = line * piece
    whole = [pl.BlockSpec(a.shape, lambda j, s: (0, 0, 0)) for a in acts]
    tile = pl.BlockSpec((3, rows, block), lambda j, s: (0, 0, j))
    weight = pl.BlockSpec(
        (line, 1, piece, width), lambda j, s: (0, jnp.where(j < PARTS, s[0], 1 - s[0]), j % PARTS, 0)
    )
    return pl.pallas_call(
        kernel,
        grid_spec=pltpu.PrefetchScalarGridSpec(
            num_scalar_prefetch=1,
            grid=(2 * PARTS,),
            in_specs=whole + [tile] * len(tiles) + [weight] * len(weights),
            out_specs=[tile] * out_count,
        ),
        out_shape=[jax.ShapeDtypeStruct((3, rows, 2 * line * owned), BF)] * out_count,
        compiler_params=pltpu.CompilerParams(vmem_limit_bytes=VMEM),
        cost_estimate=pl.CostEstimate(flops=cost, bytes_accessed=cost // 400, transcendentals=0),
    )(side, *acts, *tiles, *weights)


def model_call(kernel, side, acts, weights, block, cost):
    line, _, owned, width = weights[0].shape
    rows = acts[0].shape[1]
    whole = [pl.BlockSpec(a.shape, lambda j, s: (0, 0, 0)) for a in acts]
    weight = pl.BlockSpec((line, 2, owned, block), lambda j, s: (0, 0, 0, j))
    out = pl.BlockSpec((3, rows // 2, block), lambda j, s: (0, 0, j))
    return pl.pallas_call(
        kernel,
        grid_spec=pltpu.PrefetchScalarGridSpec(
            num_scalar_prefetch=1,
            grid=(width // block,),
            in_specs=whole + [weight] * len(weights),
            out_specs=[out, out],
        ),
        out_shape=[jax.ShapeDtypeStruct((3, rows // 2, width), BF)] * 2,
        compiler_params=pltpu.CompilerParams(vmem_limit_bytes=VMEM),
        cost_estimate=pl.CostEstimate(flops=cost, bytes_accessed=cost // 400, transcendentals=0),
    )(side, *acts, *weights)


def weight_rows(ref):
    line, _, piece, width = ref.shape
    return ref[...].reshape(line * piece, width)


def weight_columns(side, ref):
    line, _, owned, _ = ref.shape
    piece = owned // PARTS
    return jnp.concatenate(
        [
            ref[place, which, part * piece : (part + 1) * piece, :]
            for which in (side, 1 - side)
            for part in range(PARTS)
            for place in range(line)
        ],
        axis=0,
    )


def gate_up_kernel(scale, side_ref, n2_ref, gate_ref, up_ref, hid_ref, slope_gate_ref, slope_up_ref):
    gates, ups = all_codes(weight_rows(gate_ref)), all_codes(weight_rows(up_ref))
    for w in range(3):
        n2 = n2_ref[w]
        gate = dot_rows(n2, gates[w]) * (scale * STEP[w])
        up = dot_rows(n2, ups[w]) * (scale * STEP[w])
        act, slope = gelu_parts(gate)
        hid_ref[w] = (act * up).astype(BF)
        slope_gate_ref[w] = (up * slope).astype(BF)
        slope_up_ref[w] = act.astype(BF)


def down_kernel(scale, side_ref, hid_ref, down_ref, first_ref, second_ref):
    half = first_ref.shape[1]
    for w, code in enumerate(all_codes(weight_columns(side_ref[0], down_ref))):
        part = (dot(hid_ref[w], code) * (scale * STEP[w])).astype(BF)
        first_ref[w] = part[:half]
        second_ref[w] = part[half:]


def d_hidden_kernel(scale, side_ref, d_ff_ref, slope_gate_ref, slope_up_ref, down_ref, d_gate_ref, d_up_ref):
    for w, code in enumerate(all_codes(weight_rows(down_ref))):
        d_hid = (dot_rows(d_ff_ref[w], code) * (scale * STEP[w])).astype(BF).astype(F32)
        d_gate_ref[w] = (d_hid * slope_gate_ref[w].astype(F32)).astype(BF)
        d_up_ref[w] = (d_hid * slope_up_ref[w].astype(F32)).astype(BF)


def d_model_kernel(scale, side_ref, d_gate_ref, d_up_ref, gate_ref, up_ref, first_ref, second_ref):
    half = first_ref.shape[1]
    gates = all_codes(weight_columns(side_ref[0], gate_ref))
    ups = all_codes(weight_columns(side_ref[0], up_ref))
    for w in range(3):
        part = dot(d_gate_ref[w], gates[w]) + dot(d_up_ref[w], ups[w])
        part = (part * (scale * STEP[w])).astype(BF)
        first_ref[w] = part[:half]
        second_ref[w] = part[half:]


def make_body(seq_size):
    line = seq_size // 2
    core_pairs = [(i, i ^ 1) for i in range(4)]
    far_pairs = [(i, i ^ 2) for i in range(4)]
    side_pairs = [(i, i ^ 1) for i in range(seq_size)]

    def core_swap(value):
        return lax.ppermute(value, "head", core_pairs)

    def far_swap(value):
        return lax.ppermute(value, "head", far_pairs)

    def side_swap(value):
        return lax.ppermute(value, "seq", side_pairs)

    def line_shift(value, hops):
        pairs = [(i, i + 2 * hops) for i in range(seq_size) if 0 <= i + 2 * hops < seq_size]
        return lax.ppermute(value, "seq", pairs)

    def line_turn(value, hops):
        return lax.ppermute(value, "seq", [(i, (i + 2 * hops) % seq_size) for i in range(seq_size)])

    def reduce_head(part):
        half = part.shape[1] // 2
        return reduce_halves(part[:, :half], part[:, half:].astype(BF))

    def reduce_halves(kept, sent):
        quarter = kept.shape[1] // 2
        both = kept.astype(F32) + core_swap(sent).astype(F32)
        got = far_swap(both[:, quarter:].astype(BF))
        return both[:, :quarter] + got.astype(F32)

    def gather_head(own):
        two = jnp.concatenate([own, far_swap(own)], axis=1)
        return jnp.concatenate([two, core_swap(two)], axis=1)

    lines = [list(range(first, seq_size, 2)) for first in range(2)]

    def line_scatter(chunks):
        return lax.psum_scatter(
            chunks, "seq", scatter_dimension=0, axis_index_groups=lines, tiled=True
        ).astype(F32)

    def body(
        tokens, cotangent, doc_lengths, pad_mask, gain_one, gain_two, gain_three, gain_four,
        w_query, w_key, w_value, w_out, w_gate, w_up, w_down,
    ):
        rows, width = tokens.shape
        quarter = rows // 4
        heads = w_query.shape[0] // HD
        hidden = w_gate.shape[0]
        head_all, hidden_all = 4 * w_query.shape[0], 4 * hidden
        sm = 1.0 / (64.0 * math.sqrt(width))
        so = 1.0 / (64.0 * math.sqrt(head_all))
        sf = 1.0 / (64.0 * math.sqrt(hidden_all))
        root_scale = 1.0 / math.sqrt(HD)
        h, s = lax.axis_index("head"), lax.axis_index("seq")
        place, side = s // 2, s % 2
        orders = [h, h ^ 2, h ^ 1, h ^ 3]

        def relative(value):
            return jnp.concatenate(
                [lax.dynamic_slice_in_dim(value, o * quarter, quarter, 0) for o in orders], axis=0
            )

        def natural(value):
            parts = []
            for block in range(4):
                bits = h ^ block
                slot = (bits % 2) * 2 + bits // 2
                parts.append(lax.dynamic_slice_in_dim(value, slot * quarter, quarter, 1))
            return jnp.concatenate(parts, axis=1)

        x_all = relative(tokens).astype(F32)
        x_own = x_all[:quarter]
        dy_own = lax.dynamic_slice_in_dim(cotangent, h * quarter, quarter, 1)
        within = jnp.concatenate(
            [o * quarter + jnp.arange(quarter, dtype=jnp.int32) for o in orders], axis=0
        )
        position = s * rows + within
        segment, turn = doc_info(position, doc_lengths)
        freq = jnp.exp(jnp.arange(HD // 2, dtype=F32) * (-2.0 * math.log(10000.0) / HD))
        angle = turn.astype(F32)[:, None] * freq[None, :]
        cosine, sine = jnp.cos(angle), jnp.sin(angle)

        inverse_one = inverse_rms(x_all)
        n1 = (x_all * inverse_one * gain_one).astype(BF)
        master_qkv = jnp.concatenate([w_query, w_key, w_value], axis=0)
        gate_rows, up_rows, down_rows = (
            w.reshape(line, 2, hidden // seq_size, width) for w in (w_gate, w_up, w_down)
        )
        which_side = jnp.reshape(side, (1,)).astype(jnp.int32)

        half_rows = rows // 2
        pad_row = relative(pad_mask).astype(BF)[None, :]
        pad_block = jnp.pad(pad_row, ((0, 15), (0, width - rows)))
        packed = jnp.concatenate([n1[:half_rows], pad_block], axis=0)
        near = [packed] + [line_turn(packed, hops) for hops in range(1, line)]
        pieces, valid, key_position = [], [], []
        for hops in range(line):
            pair = [near[hops], side_swap(near[hops])]
            other = core_swap(jnp.concatenate([b[:half_rows] for b in pair], axis=0))
            for slot, which in ((0, side), (1, 1 - side)):
                pieces += [pair[slot][:half_rows], other[slot * half_rows : (slot + 1) * half_rows]]
                valid.append(pair[slot][half_rows, :rows])
                key_position.append((2 * ((place - hops) % line) + which) * rows + within)
        n1_all = jnp.concatenate(pieces, axis=0)
        key_position = jnp.concatenate(key_position, axis=0)
        key_valid = jnp.concatenate(valid, axis=0) > 0.5
        key_segment, key_turn = doc_info(key_position, doc_lengths)
        key_angle = key_turn.astype(F32)[:, None] * freq[None, :]
        key_cosine, key_sine = jnp.cos(key_angle), jnp.sin(key_angle)
        allowed = (
            (segment[:, None] == key_segment[None, :])
            & (key_position[None, :] <= position[:, None])
            & (key_valid[None, :] | (key_position[None, :] == position[:, None]))
        )
        allowed = jnp.concatenate([allowed] * heads, axis=0)
        master_kv = jnp.concatenate([w_key, w_value], axis=0)

        queries, keys, values, probs, slopes, contexts, part_attn = [], [], [], [], [], [], []
        for w in range(3):
            query = dot_rows(n1, codes(w_query, w)) * (sm * STEP[w])
            queries.append(
                jnp.concatenate(
                    [rotate(query[:, j * HD : (j + 1) * HD], cosine, sine) for j in range(heads)], axis=0
                ).astype(BF)
            )
            kv = dot_rows(n1_all, codes(master_kv, w)) * (sm * STEP[w])
            key = rotate(kv[:, :HD], key_cosine, key_sine).astype(BF)
            value = kv[:, HD:].astype(BF)
            bend = jnp.tanh(dot_rows(queries[w], key) * (root_scale / SOFTCAP))
            expo = jnp.where(allowed, jnp.exp(SOFTCAP * bend), 0.0)
            weight = expo / jnp.sum(expo, axis=1, keepdims=True)
            prob = weight.astype(BF)
            slope = (weight * (1.0 - bend * bend) * root_scale).astype(BF)
            context = dot(prob, value).astype(BF)
            context = jnp.concatenate(
                [context[j * rows : (j + 1) * rows] for j in range(heads)], axis=1
            )
            keys.append(key)
            values.append(value)
            probs.append(prob)
            slopes.append(slope)
            contexts.append(context)
            part_attn.append(dot(context, codes(w_out, w)) * (so * STEP[w]))

        def flat(value):
            return value.reshape(3 * value.shape[1], value.shape[2])

        def both_sides(value):
            got = side_swap(value[:, :half_rows])
            return jnp.concatenate([flat(value), flat(jnp.concatenate([got, core_swap(got)], axis=1))], axis=0)

        def both_halves(value):
            value = flat(value)
            return jnp.concatenate(
                [value[:, : hidden // 2], side_swap(value[:, hidden // 2 :])], axis=0
            )

        def weight_grad(left, right, scale):
            total = (dot_cols(left, right) * scale).astype(BF)
            owned = hidden // seq_size
            total = total.reshape(PARTS, line, owned // PARTS, width).swapaxes(0, 1)
            return line_scatter(total.reshape(line * owned, width))

        attn = reduce_head(jnp.stack(part_attn))
        inverse_two = inverse_rms(attn)
        middle = x_own + attn * inverse_two * gain_two
        inverse_three = inverse_rms(middle)
        n2 = gather_head((middle * inverse_three * gain_three).astype(BF))
        cost = 6 * rows * hidden * width
        hid, slope_gate, slope_up = hidden_call(
            functools.partial(gate_up_kernel, sm), which_side, [n2], [], [gate_rows, up_rows], 3, 2 * cost
        )
        right_gate = both_sides(n2)
        ff = reduce_halves(
            *model_call(functools.partial(down_kernel, sf), which_side, [hid], [down_rows], 384, cost)
        )
        left_down = both_halves(hid)
        inverse_four = inverse_rms(ff)
        dy = dy_own.astype(F32)
        result = (middle + ff * inverse_four * gain_four).astype(BF)
        d_ff_own, sums_four = rms_back(flat(ff), flat(inverse_four), gain_four, flat(dy))
        d_ff = gather_head(d_ff_own.astype(BF).reshape(3, quarter, width))
        right_down = both_sides(d_ff)
        d_gate, d_up = hidden_call(
            functools.partial(d_hidden_kernel, sf), which_side, [d_ff], [slope_gate, slope_up],
            [down_rows], 2, cost,
        )
        grad_down = weight_grad(left_down, right_down, sf)
        d_n2 = flat(
            reduce_halves(
                *model_call(
                    functools.partial(d_model_kernel, sm), which_side, [d_gate, d_up],
                    [gate_rows, up_rows], 384, 2 * cost,
                )
            )
        )
        left_gate, left_up = both_halves(d_gate), both_halves(d_up)
        grad_gate = weight_grad(left_gate, right_gate, sm)
        grad_up = weight_grad(left_up, right_gate, sm)
        d_norm, sums_three = rms_back(flat(middle), flat(inverse_three), gain_three, d_n2)
        d_middle = flat(dy) + d_norm
        d_attn_own, sums_two = rms_back(flat(attn), flat(inverse_two), gain_two, d_middle)
        middle_grads = jnp.sum(d_middle.reshape(3, quarter, width), axis=0)
        d_attns = gather_head(d_attn_own.astype(BF).reshape(3, quarter, width))
        activations = natural(gather_head(result))

        d_qs, d_blocks = [], []
        for w in range(3):
            d_context = (dot_rows(d_attns[w], codes(w_out, w)) * (so * STEP[w])).astype(BF)
            d_context = jnp.concatenate(
                [d_context[:, j * HD : (j + 1) * HD] for j in range(heads)], axis=0
            )
            d_prob = dot_rows(d_context, values[w])
            delta = jnp.sum(probs[w].astype(F32) * d_prob, axis=1, keepdims=True)
            d_score = (slopes[w].astype(F32) * (d_prob - delta)).astype(BF)
            d_q = dot(d_score, keys[w]).astype(BF).astype(F32)
            d_qs.append(
                jnp.concatenate(
                    [rotate(d_q[j * rows : (j + 1) * rows], cosine, -sine) for j in range(heads)], axis=1
                ).astype(BF)
            )
            d_key = dot_cols(d_score, queries[w])
            d_value = dot_cols(probs[w], d_context)
            d_blocks.append(
                jnp.concatenate([d_key, d_value], axis=1).reshape(line, 2, rows, 2 * HD)
            )
        d_block = jnp.stack(d_blocks, axis=1)
        got = side_swap(d_block[:, :, 1].astype(BF))
        d_block = d_block[:, :, 0] + got.astype(F32)
        d_kv = d_block[0]
        for hops in range(1, line):
            d_kv = d_kv + line_shift(d_block[hops].astype(BF), -hops).astype(F32)
        d_qkv = []
        part_n1 = jnp.zeros((rows, width), F32)
        for w in range(3):
            d_key = d_kv[w, :, :HD].astype(BF).astype(F32)
            d_qkv.append(
                jnp.concatenate(
                    [d_qs[w], rotate(d_key, cosine, -sine).astype(BF), d_kv[w, :, HD:].astype(BF)], axis=1
                )
            )
            part_n1 = part_n1 + dot(d_qkv[w], codes(master_qkv, w)) * (sm * STEP[w])
        d_n1 = reduce_head(part_n1[None])[0]
        d_norm, sums_one = rms_back(x_own, inverse_one[:quarter], gain_one, d_n1)
        grad_tokens = natural(gather_head((middle_grads + d_norm).astype(BF)[None]))[0]

        owned_out = w_out.shape[0] // seq_size
        term = dot_cols(jnp.concatenate(contexts, axis=0), flat(d_attns)) * so
        term = term.reshape(line, 2, owned_out, width)
        got = side_swap(lax.dynamic_index_in_dim(term, 1 - side, 1, keepdims=False).astype(BF))
        term = lax.dynamic_index_in_dim(term, side, 1, keepdims=False) + got.astype(F32)
        grad_out = line_scatter(term.reshape(line * owned_out, width).astype(BF))

        d_sum = (d_qkv[0].astype(F32) + d_qkv[1].astype(F32) + d_qkv[2].astype(F32)).astype(BF).T
        cuts = [w_query.shape[0], w_key.shape[0], w_value.shape[0]]
        sent, begin = [], 0
        for cut in cuts:
            sent.append(d_sum[begin : begin + cut].reshape(seq_size, cut // seq_size, rows))
            begin += cut
        sent = jnp.concatenate(sent, axis=1)
        owned_qkv = sent.shape[1]
        sent = sent.swapaxes(1, 2).reshape(line, 2, rows, owned_qkv)
        other = side_swap(lax.dynamic_index_in_dim(sent, 1 - side, 1, keepdims=False))
        own = lax.dynamic_index_in_dim(sent, side, 1, keepdims=False)
        both = jnp.stack([own, other], axis=1)
        arrived = []
        for hops in range(line):
            chunk = lax.dynamic_index_in_dim(both, (place + hops) % line, 0, keepdims=False)
            chunk = line_turn(chunk, hops) if hops else chunk
            arrived.append(chunk.reshape(2 * rows, owned_qkv))
        total = dot_cols(jnp.concatenate(arrived, axis=0), n1_all)
        total = total * sm
        cut_q, cut_k = cuts[0] // seq_size, cuts[1] // seq_size
        grad_query, grad_key, grad_value = (
            total[:cut_q], total[cut_q : cut_q + cut_k], total[cut_q + cut_k :],
        )

        sums = jnp.concatenate([sums_one, sums_two, sums_three, sums_four], axis=0)
        sums = sums + core_swap(sums)
        sums = sums + far_swap(sums)
        bit = 1
        while bit < seq_size:
            sums = sums + lax.ppermute(sums, "seq", [(i, i ^ bit) for i in range(seq_size)])
            bit *= 2
        share = width // seq_size
        sums = lax.dynamic_slice_in_dim(sums, s * share, share, 1)
        return (
            activations, grad_tokens, grad_query, grad_key, grad_value, grad_out, grad_gate, grad_up,
            grad_down, sums[0], sums[1], sums[2], sums[3],
        )

    return body


def solution(mesh):
    row, rep, vec = P("head", None), P(), P("seq")
    in_specs = (P("seq", None), P(None, "seq", None), rep, vec, rep, rep, rep, rep) + (row,) * 7
    both = P(("head", "seq"), None)
    out_specs = (P(None, "seq", None), P("seq", None)) + (both,) * 7 + (vec,) * 4
    return jax.shard_map(
        make_body(mesh.shape["seq"]), mesh=mesh, in_specs=in_specs, out_specs=out_specs, check_vma=False
    )
```

time: 961 us -> 818 us (0.85)
  matrix products: 239 us -> 85.4 us
  starting transfers between devices: 160 us -> 43.2 us
  waiting for transfers between devices: 337 us -> 421 us
  Pallas kernels: 0 us -> 78.9 us
  other arithmetic: 105 us -> 82 us
  local copies, waits for them, and re-layouts: 94.3 us -> 82.8 us
    ppermute x30 -> x3, starting transfers between devices: 126 us -> 3.88 us  [line_shift(): return lax.ppermute(value, 'seq', pairs)]
    ppermute x12, waiting for transfers between devices: 61.5 us -> 177 us  [side_swap(): return lax.ppermute(value, 'seq', side_pairs)]
    dot_general x21 -> x15, matrix products: 111 us -> 28.6 us  [dot_rows(): lax.dot_general(left, right, (((1,), (1,)), ((), ())), preferred_element_...]
    ppermute x30 -> x3, waiting for transfers between devices: 188 us -> 109 us  [line_shift(): return lax.ppermute(value, 'seq', pairs)]
    pallas_call x0 -> x4, Pallas kernels: none -> 78.9 us  [the longest x2 43 us: hidden_call(): pl.pallas_call(kernel, grid_spec=pltpu.PrefetchScalarGridSpec(num_scalar_...]
    dot_general x29 -> x12, matrix products: 85.8 us -> 19 us  [dot(): lax.dot_general(left, right, (((1,), (0,)), ((), ())), preferred_element_...]
    ppermute x10, waiting for transfers between devices: 72.7 us -> 106 us  [far_swap(): return lax.ppermute(value, 'head', far_pairs)]
    dynamic_slice x5 -> x0, local copies, waits for them, and re-layouts: 21.9 us -> none  [the longest x2 21.6 us: halves(): lax.dynamic_index_in_dim(parts, which, 1, keepdims=False)]
  transfers between devices with their start and end apart: 71 -> 54, of which waited for: 32 -> 35; matrix products, arithmetic and copies ran while one was open for 31% -> 21% of each run, Pallas kernels for 0% -> 0%
where the time goes in v3:
time: 818 us; the launch traced here: 810 us
  waiting for transfers between devices  421 us (51%)
  matrix products  85.4 us (10%)
  local copies, waits for them, and re-layouts  82.8 us (10%)
  other arithmetic  82 us (10%)
  Pallas kernels  78.9 us (10%)
  starting transfers between devices  43.2 us (5%)
  between operations  16.1 us (2%)
    ppermute x12, waiting for transfers between devices, side_swap(): return lax.ppermute(value, 'seq', side_pairs)  177 us
    ppermute x3, waiting for transfers between devices, line_shift(): return lax.ppermute(value, 'seq', pairs)  109 us
    ppermute x10, waiting for transfers between devices, far_swap(): return lax.ppermute(value, 'head', far_pairs)  106 us
    pallas_call x2, Pallas kernels, hidden_call(): pl.pallas_call(kernel, grid_spec=pltpu.PrefetchScalarGridSpec(num_scalar_...  43 us
    dot_general x11, matrix products, dot_cols(): lax.dot_general(left, right, (((0,), (0,)), ((), ())), preferred_element_...  37.8 us
    pallas_call x2, Pallas kernels, model_call(): pl.pallas_call(kernel, grid_spec=pltpu.PrefetchScalarGridSpec(num_scalar_...  35.9 us
    unnamed x273, local copies, waits for them, and re-layouts  33.3 us
    dot_general x15, matrix products, dot_rows(): lax.dot_general(left, right, (((1,), (1,)), ((), ())), preferred_element_...  28.6 us
  transfers between devices with their start and end apart: 54, of which 35 were waited for; matrix products, arithmetic and copies ran while one was open for 21% of the time, Pallas kernels for 0%

profile of v3, /device:TPU:0, one launch (start us, length us, event | category | flops | bytes accessed | tf_op | source)
XLA Modules:
  0.0 809.6 jit_solution(13493496379846244149)
XLA Ops:
  20.3 6.1 collective-permute-done
  33.7 9.3 %collective-permute-done.2 = bf16[112,2304]{1,0:T(8,128)(2,1)S(1)} collective-permute-done((bf16[112,2304]{1,0:T(8,128)(2,1)}, bf16[112,2304]{1,0:T(8,128)(2,1)S(1)}, u32[]{:S(2)}, u32[]{:S(2)}) %collective-permute-start.2) | collective-permute-done | bytes 516128 | tf_op jit(solution)/shard_map/ppermute | solution.py:204
  56.6 9.3 %collective-permute-done.4 = bf16[112,2304]{1,0:T(8,128)(2,1)S(1)} collective-permute-done((bf16[112,2304]{1,0:T(8,128)(2,1)}, bf16[112,2304]{1,0:T(8,128)(2,1)S(1)}, u32[]{:S(2)}, u32[]{:S(2)}) %collective-permute-start.4) | collective-permute-done | bytes 516128 | tf_op jit(solution)/shard_map/ppermute | solution.py:204
  75.3 11.7 %collective-permute-done.6 = bf16[112,2304]{1,0:T(8,128)(2,1)S(1)} collective-permute-done((bf16[112,2304]{1,0:T(8,128)(2,1)}, bf16[112,2304]{1,0:T(8,128)(2,1)S(1)}, u32[]{:S(2)}, u32[]{:S(2)}) %collective-permute-start.6) | collective-permute-done | bytes 516128 | tf_op jit(solution)/shard_map/ppermute | solution.py:204
  99.5 7.2 convolution_multiply_fusion.10
  106.8 3.9 convolution_multiply_fusion.8
  110.6 3.9 convolution_multiply_fusion.9
  136.9 15.3 %collective-permute-done.12 = bf16[3,48,2304]{2,1,0:T(8,128)(2,1)S(1)} collective-permute-done((bf16[3,48,2304]{2,1,0:T(8,128)(2,1)S(1)}, bf16[3,48,2304]{2,1,0:T(8,128)(2,1)S(1)}, u32[]{:S(2)}, u32[]{:S(2)}) %collective-permute-start.12) | collective-permute-done | bytes 663584 | tf_op jit(solution)/shard_map/ppermute | solution.py:201
  154.9 14.6 %collective-permute-done.13 = bf16[3,48,2304]{2,1,0:T(8,128)(2,1)S(1)} collective-permute-done((bf16[3,48,2304]{2,1,0:T(8,128)(2,1)S(1)}, bf16[3,48,2304]{2,1,0:T(8,128)(2,1)S(1)}, u32[]{:S(2)}, u32[]{:S(2)}) %collective-permute-start.13) | collective-permute-done | bytes 663584 | tf_op jit(solution)/shard_map/ppermute | solution.py:201
  175.5 27.4 %shard_map.246 = (bf16[3,192,2304]{2,1,0:T(8,128)(2,1)}, bf16[3,192,2304]{2,1,0:T(8,128)(2,1)}, bf16[3,192,2304]{2,1,0:T(8,128)(2,1)}) custom-call(s32[1]{0:T(128)} %bitcast.7.side_ref, bf16[3,192,2304]{2,1,0:T(8,128)(2,1)} %pad_maximum_fusion.9.n2_ref, bf16[4,2,288,2304]{3,2,1,0:T(8,128)(2,1)} %bitcast.197, bf16[4,2,288,2304]{3,2,1,0:T(8,128)(2,1)} %bitcast.199), custom_call_target="tpu_custom_call" | custom-call | flops 12230590464 | bytes 30576476 | tf_op jit(solution)/shard_map/pallas_call | solution.py:100
  202.9 13.1 %shard_map.247 = (bf16[3,96,2304]{2,1,0:T(8,128)(2,1)}, bf16[3,96,2304]{2,1,0:T(8,128)(2,1)}) custom-call(s32[1]{0:T(128)} %bitcast.7.side_ref, bf16[3,192,2304]{2,1,0:T(8,128)(2,1)} %get-tuple-element.22.hid_ref, bf16[4,2,288,2304]{3,2,1,0:T(8,128)(2,1)} %bitcast.195), custom_call_target="tpu_custom_call" | custom-call | flops 6115295232 | bytes 15288238 | tf_op jit(solution)/shard_map/pallas_call | solution.py:120
  222.6 15.5 %collective-permute-done.16 = bf16[3,48,2304]{2,1,0:T(8,128)(2,1)S(1)} collective-permute-done((bf16[3,48,2304]{2,1,0:T(8,128)(2,1)S(1)}, bf16[3,48,2304]{2,1,0:T(8,128)(2,1)S(1)}, u32[]{:S(2)}, u32[]{:S(2)}) %collective-permute-start.16) | collective-permute-done | bytes 663584 | tf_op jit(solution)/shard_map/ppermute | solution.py:201
  242.4 14.6 %collective-permute-done.19 = bf16[3,48,2304]{2,1,0:T(8,128)(2,1)S(1)} collective-permute-done((bf16[3,48,2304]{2,1,0:T(8,128)(2,1)S(1)}, bf16[3,48,2304]{2,1,0:T(8,128)(2,1)S(1)}, u32[]{:S(2)}, u32[]{:S(2)}) %collective-permute-start.19) | collective-permute-done | bytes 663584 | tf_op jit(solution)/shard_map/ppermute | solution.py:201
  263.1 15.6 %shard_map.248 = (bf16[3,192,2304]{2,1,0:T(8,128)(2,1)}, bf16[3,192,2304]{2,1,0:T(8,128)(2,1)}) custom-call(s32[1]{0:T(128)} %bitcast.7.side_ref, bf16[3,192,2304]{2,1,0:T(8,128)(2,1)} %pad_maximum_fusion.12.d_ff_ref, bf16[3,192,2304]{2,1,0:T(8,128)(2,1)} %get-tuple-element.25.slope_gate_ref, bf16[3,192,2304]{2,1,0:T(8,128)(2,1)} %get-tuple-element.26.slope_up_ref, ...), custom_call_target="tpu_custom_call" | custom-call | flops 6115295232 | bytes 15288238 | tf_op jit(solution)/shard_map/pallas_call | solution.py:100
  278.7 22.7 %shard_map.249 = (bf16[3,96,2304]{2,1,0:T(8,128)(2,1)}, bf16[3,96,2304]{2,1,0:T(8,128)(2,1)}) custom-call(s32[1]{0:T(128)} %bitcast.7.side_ref, bf16[3,192,2304]{2,1,0:T(8,128)(2,1)} %get-tuple-element.27.d_gate_ref, bf16[3,192,2304]{2,1,0:T(8,128)(2,1)} %get-tuple-element.28.d_up_ref, bf16[4,2,288,2304]{3,2,1,0:T(8,128)(2,1)} %bitcast.198, ...), custom_call_target="tpu_custom_call" | custom-call | flops 12230590464 | bytes 30576476 | tf_op jit(solution)/shard_map/pallas_call | solution.py:120
  308.1 15.5 %collective-permute-done.22 = bf16[3,48,2304]{2,1,0:T(8,128)(2,1)S(1)} collective-permute-done((bf16[3,48,2304]{2,1,0:T(8,128)(2,1)S(1)}, bf16[3,48,2304]{2,1,0:T(8,128)(2,1)S(1)}, u32[]{:S(2)}, u32[]{:S(2)}) %collective-permute-start.22) | collective-permute-done | bytes 663584 | tf_op jit(solution)/shard_map/ppermute | solution.py:201
  329.5 14.6 %collective-permute-done.23 = bf16[3,48,2304]{2,1,0:T(8,128)(2,1)S(1)} collective-permute-done((bf16[3,48,2304]{2,1,0:T(8,128)(2,1)S(1)}, bf16[3,48,2304]{2,1,0:T(8,128)(2,1)S(1)}, u32[]{:S(2)}, u32[]{:S(2)}) %collective-permute-start.23) | collective-permute-done | bytes 663584 | tf_op jit(solution)/shard_map/ppermute | solution.py:201
  355.9 21.6 %collective-permute-done.43 = bf16[3,96,2304]{2,1,0:T(8,128)(2,1)} collective-permute-done((bf16[3,96,2304]{2,1,0:T(8,128)(2,1)}, bf16[3,96,2304]{2,1,0:T(8,128)(2,1)}, u32[]{:S(2)}, u32[]{:S(2)}) %collective-permute-start.43) | collective-permute-done | bytes 1327136 | tf_op jit(solution)/shard_map/ppermute | solution.py:204
  381.6 21.2 %collective-permute-done.37 = bf16[4,64,2304]{2,1,0:T(8,128)(2,1)} collective-permute-done((bf16[4,64,2304]{2,1,0:T(8,128)(2,1)}, bf16[4,64,2304]{2,1,0:T(8,128)(2,1)}, u32[]{:S(2)}, u32[]{:S(2)}) %collective-permute-start.37) | collective-permute-done | bytes 1179680 | tf_op jit(solution)/shard_map/ppermute | solution.py:204
  407.5 23.3 %collective-permute-done.42 = bf16[576,1152]{1,0:T(8,128)(2,1)} collective-permute-done((bf16[576,1152]{1,0:T(8,128)(2,1)}, bf16[576,1152]{1,0:T(8,128)(2,1)}, u32[]{:S(2)}, u32[]{:S(2)}) %collective-permute-start.42) | collective-permute-done | bytes 1327136 | tf_op jit(solution)/shard_map/ppermute | solution.py:204
  430.8 9.0 %fusion.2 = bf16[1152,2304]{1,0:T(8,128)(2,1)S(1)} fusion(bf16[576,2304]{1,0:T(8,128)(2,1)S(1)} %bitcast.182, bf16[576,2304]{1,0:T(8,128)(2,1)S(1)} %bitcast.181, bf16[576,1152]{1,0:T(8,128)(2,1)} %collective-permute-done.42, bf16[576,1152]{1,0:T(8,128)(2,1)S(1)} %copy-done.50), kind=kOutput, calls=%fused_computation.5 | convolution fusion | flops 6136528896 | bytes 13271040 | tf_op jit(solution)/shard_map/dot_general | solution.py:34
  443.2 30.6 %collective-permute-done.39 = bf16[3,96,2304]{2,1,0:T(8,128)(2,1)} collective-permute-done((bf16[3,96,2304]{2,1,0:T(8,128)(2,1)}, bf16[3,96,2304]{2,1,0:T(8,128)(2,1)}, u32[]{:S(2)}, u32[]{:S(2)}) %collective-permute-start.39) | collective-permute-done | bytes 1327136 | tf_op jit(solution)/shard_map/ppermute | solution.py:204
  480.2 11.3 %collective-permute-done.17 = bf16[3,48,2304]{2,1,0:T(8,128)(2,1)S(1)} collective-permute-done((bf16[3,48,2304]{2,1,0:T(8,128)(2,1)S(1)}, bf16[3,48,2304]{2,1,0:T(8,128)(2,1)S(1)}, u32[]{:S(2)}, u32[]{:S(2)}) %collective-permute-start.17) | collective-permute-done | bytes 663584 | tf_op jit(solution)/shard_map/ppermute | solution.py:201
  495.0 14.8 %collective-permute-done.41 = bf16[576,1152]{1,0:T(8,128)(2,1)S(1)} collective-permute-done((bf16[576,1152]{1,0:T(8,128)(2,1)S(1)}, bf16[576,1152]{1,0:T(8,128)(2,1)S(1)}, u32[]{:S(2)}, u32[]{:S(2)}) %collective-permute-start.41) | collective-permute-done | bytes 1327136 | tf_op jit(solution)/shard_map/ppermute | solution.py:204
  509.7 7.7 fusion.1
  535.8 4.3 multiply_convert_fusion.4
  562.2 3.8 pad_maximum_fusion
  571.1 10.1 %fusion = bf16[1152,2304]{1,0:T(8,128)(2,1)S(1)} fusion(bf16[576,2304]{1,0:T(8,128)(2,1)} %bitcast.180, bf16[576,2304]{1,0:T(8,128)(2,1)S(1)} %bitcast.175, bf16[576,1152]{1,0:T(8,128)(2,1)} %collective-permute-done.38, bf16[576,1152]{1,0:T(8,128)(2,1)S(1)} %copy-done.49), kind=kOutput, calls=%fused_computation.3 | convolution fusion | flops 6136528896 | bytes 13271040 | tf_op jit(solution)/shard_map/dot_general | solution.py:34
  593.3 27.1 %collective-permute-done.25 = bf16[4,3,192,512]{3,2,1,0:T(8,128)(2,1)} collective-permute-done((bf16[4,3,192,512]{3,2,1,0:T(8,128)(2,1)}, bf16[4,3,192,512]{3,2,1,0:T(8,128)(2,1)}, u32[]{:S(2)}, u32[]{:S(2)}) %collective-permute-start.25) | collective-permute-done | bytes 2359328 | tf_op jit(solution)/shard_map/ppermute | solution.py:204
  628.7 33.5 %collective-permute-done.26 = bf16[3,192,512]{2,1,0:T(8,128)(2,1)S(1)} collective-permute-done((bf16[3,192,512]{2,1,0:T(8,128)(2,1)S(1)}, bf16[3,192,512]{2,1,0:T(8,128)(2,1)S(1)}, u32[]{:S(2)}, u32[]{:S(2)}) %collective-permute-start.26) | collective-permute-done | bytes 589856 | tf_op jit(solution)/shard_map/ppermute | solution.py:208
  662.3 75.7 %collective-permute-done.27 = bf16[3,192,512]{2,1,0:T(8,128)(2,1)S(1)} collective-permute-done((bf16[3,192,512]{2,1,0:T(8,128)(2,1)S(1)}, bf16[3,192,512]{2,1,0:T(8,128)(2,1)S(1)}, u32[]{:S(2)}, u32[]{:S(2)}) %collective-permute-start.27) | collective-permute-done | bytes 589856 | tf_op jit(solution)/shard_map/ppermute | solution.py:208
  780.5 4.1 convolution_multiply_fusion.7
  (549 shorter events, 274.8 us)
Async XLA Ops:
  7.2 783.0 %reduce-scatter.5.cloned.1.call-start = ((), (), s32[]{:S(2)}) async-start(), calls=%async_computation.4 | async-start | bytes 1474560 | tf_op jit(solution)/shard_map/reduce_scatter | solution.py:230
  11.6 14.9 %collective-permute-start = (bf16[112,2304]{1,0:T(8,128)(2,1)}, bf16[112,2304]{1,0:T(8,128)(2,1)S(1)}, u32[]{:S(2)}, u32[]{:S(2)}) collective-permute-start(bf16[112,2304]{1,0:T(8,128)(2,1)} %pad_maximum_fusion.33), channel_id=1, source_target_pairs={{0,1},{1,0},{2,3},{3,2},{4,5},{5,4},{6,7},{7,6},{8,9},{9,8},{10,11... | collective-permute-start | bytes 1548296 | tf_op jit(solution)/shard_map/ppermute | solution.py:204
  14.5 16.9 %collective-permute-start.1 = (bf16[112,2304]{1,0:T(8,128)(2,1)}, bf16[112,2304]{1,0:T(8,128)(2,1)}, u32[]{:S(2)}, u32[]{:S(2)}) collective-permute-start(bf16[112,2304]{1,0:T(8,128)(2,1)} %pad_maximum_fusion.33), channel_id=1, source_target_pairs={{0,2},{1,3},{2,4},{3,5},{4,6},{5,7},{6,0},{7,1},{8,10},{9,11},{10,... | collective-permute-start | bytes 1548296 | tf_op jit(solution)/shard_map/ppermute | solution.py:211
  16.1 36.1 %collective-permute-start.3 = (bf16[112,2304]{1,0:T(8,128)(2,1)}, bf16[112,2304]{1,0:T(8,128)(2,1)}, u32[]{:S(2)}, u32[]{:S(2)}) collective-permute-start(bf16[112,2304]{1,0:T(8,128)(2,1)} %pad_maximum_fusion.33), channel_id=1, source_target_pairs={{0,4},{1,5},{2,6},{3,7},{4,0},{5,1},{6,2},{7,3},{8,12},{9,13},{10,... | collective-permute-start | bytes 1548296 | tf_op jit(solution)/shard_map/ppermute | solution.py:211
  18.7 53.9 %collective-permute-start.5 = (bf16[112,2304]{1,0:T(8,128)(2,1)}, bf16[112,2304]{1,0:T(8,128)(2,1)}, u32[]{:S(2)}, u32[]{:S(2)}) collective-permute-start(bf16[112,2304]{1,0:T(8,128)(2,1)} %pad_maximum_fusion.33), channel_id=1, source_target_pairs={{0,6},{1,7},{2,0},{3,1},{4,2},{5,3},{6,4},{7,5},{8,14},{9,15},{10,... | collective-permute-start | bytes 1548296 | tf_op jit(solution)/shard_map/ppermute | solution.py:211
  26.6 16.4 %collective-permute-start.7 = (bf16[192,2304]{1,0:T(8,128)(2,1)S(1)}, bf16[192,2304]{1,0:T(8,128)(2,1)S(1)}, u32[]{:S(2)}, u32[]{:S(2)}) collective-permute-start(bf16[192,2304]{1,0:T(8,128)(2,1)S(1)} %pad_maximum_fusion.21), channel_id=1, source_target_pairs={{0,8},{8,0},{16,24},{24,16},{1,9},{9,1},{17,25},{25,17},{2,10},{10... | collective-permute-start | bytes 2654216 | tf_op jit(solution)/shard_map/ppermute | solution.py:198
  48.3 17.7 %collective-permute-start.8 = (bf16[192,2304]{1,0:T(8,128)(2,1)}, bf16[192,2304]{1,0:T(8,128)(2,1)}, u32[]{:S(2)}, u32[]{:S(2)}) collective-permute-start(bf16[192,2304]{1,0:T(8,128)(2,1)} %pad_maximum_fusion.22), channel_id=1, source_target_pairs={{0,8},{8,0},{16,24},{24,16},{1,9},{9,1},{17,25},{25,17},{2,10},{10... | collective-permute-start | bytes 2654216 | tf_op jit(solution)/shard_map/ppermute | solution.py:198
  72.4 14.7 %collective-permute-start.9 = (bf16[192,2304]{1,0:T(8,128)(2,1)S(1)}, bf16[192,2304]{1,0:T(8,128)(2,1)S(1)}, u32[]{:S(2)}, u32[]{:S(2)}) collective-permute-start(bf16[192,2304]{1,0:T(8,128)(2,1)S(1)} %pad_maximum_fusion.23), channel_id=1, source_target_pairs={{0,8},{8,0},{16,24},{24,16},{1,9},{9,1},{17,25},{25,17},{2,10},{10... | collective-permute-start | bytes 2654216 | tf_op jit(solution)/shard_map/ppermute | solution.py:198
  135.2 17.0 %collective-permute-start.12 = (bf16[3,48,2304]{2,1,0:T(8,128)(2,1)S(1)}, bf16[3,48,2304]{2,1,0:T(8,128)(2,1)S(1)}, u32[]{:S(2)}, u32[]{:S(2)}) collective-permute-start(bf16[3,48,2304]{2,1,0:T(8,128)(2,1)S(1)} %slice.935), channel_id=1, source_target_pairs={{0,16},{8,24},{16,0},{24,8},{1,17},{9,25},{17,1},{25,9},{2,18},{10... | collective-permute-start | bytes 1990664 | tf_op jit(solution)/shard_map/ppermute | solution.py:201
  153.4 16.2 %collective-permute-start.13 = (bf16[3,48,2304]{2,1,0:T(8,128)(2,1)S(1)}, bf16[3,48,2304]{2,1,0:T(8,128)(2,1)S(1)}, u32[]{:S(2)}, u32[]{:S(2)}) collective-permute-start(bf16[3,48,2304]{2,1,0:T(8,128)(2,1)S(1)} %multiply_convert_fusion.8), channel_id=1, source_target_pairs={{0,16},{8,24},{16,0},{24,8},{1,17},{9,25},{17,1},{25,9},{2,18},{10... | collective-permute-start | bytes 1990664 | tf_op jit(solution)/shard_map/ppermute | solution.py:201
  221.0 17.0 %collective-permute-start.16 = (bf16[3,48,2304]{2,1,0:T(8,128)(2,1)S(1)}, bf16[3,48,2304]{2,1,0:T(8,128)(2,1)S(1)}, u32[]{:S(2)}, u32[]{:S(2)}) collective-permute-start(bf16[3,48,2304]{2,1,0:T(8,128)(2,1)S(1)} %slice.934), channel_id=1, source_target_pairs={{0,16},{8,24},{16,0},{24,8},{1,17},{9,25},{17,1},{25,9},{2,18},{10... | collective-permute-start | bytes 1990664 | tf_op jit(solution)/shard_map/ppermute | solution.py:201
  240.9 16.1 %collective-permute-start.19 = (bf16[3,48,2304]{2,1,0:T(8,128)(2,1)S(1)}, bf16[3,48,2304]{2,1,0:T(8,128)(2,1)S(1)}, u32[]{:S(2)}, u32[]{:S(2)}) collective-permute-start(bf16[3,48,2304]{2,1,0:T(8,128)(2,1)S(1)} %get-tuple-element.58), channel_id=1, source_target_pairs={{0,16},{8,24},{16,0},{24,8},{1,17},{9,25},{17,1},{25,9},{2,18},{10... | collective-permute-start | bytes 1990664 | tf_op jit(solution)/shard_map/ppermute | solution.py:201
  306.5 17.0 %collective-permute-start.22 = (bf16[3,48,2304]{2,1,0:T(8,128)(2,1)S(1)}, bf16[3,48,2304]{2,1,0:T(8,128)(2,1)S(1)}, u32[]{:S(2)}, u32[]{:S(2)}) collective-permute-start(bf16[3,48,2304]{2,1,0:T(8,128)(2,1)S(1)} %slice.933), channel_id=1, source_target_pairs={{0,16},{8,24},{16,0},{24,8},{1,17},{9,25},{17,1},{25,9},{2,18},{10... | collective-permute-start | bytes 1990664 | tf_op jit(solution)/shard_map/ppermute | solution.py:201
  328.0 16.2 %collective-permute-start.23 = (bf16[3,48,2304]{2,1,0:T(8,128)(2,1)S(1)}, bf16[3,48,2304]{2,1,0:T(8,128)(2,1)S(1)}, u32[]{:S(2)}, u32[]{:S(2)}) collective-permute-start(bf16[3,48,2304]{2,1,0:T(8,128)(2,1)S(1)} %multiply_convert_fusion.7), channel_id=1, source_target_pairs={{0,16},{8,24},{16,0},{24,8},{1,17},{9,25},{17,1},{25,9},{2,18},{10... | collective-permute-start | bytes 1990664 | tf_op jit(solution)/shard_map/ppermute | solution.py:201
  345.2 32.3 %collective-permute-start.43 = (bf16[3,96,2304]{2,1,0:T(8,128)(2,1)}, bf16[3,96,2304]{2,1,0:T(8,128)(2,1)}, u32[]{:S(2)}, u32[]{:S(2)}) collective-permute-start(bf16[3,96,2304]{2,1,0:T(8,128)(2,1)} %pad_maximum_fusion.19), channel_id=1, source_target_pairs={{0,1},{1,0},{2,3},{3,2},{4,5},{5,4},{6,7},{7,6},{8,9},{9,8},{10,11... | collective-permute-start | bytes 3981320 | tf_op jit(solution)/shard_map/ppermute | solution.py:204
  355.5 47.4 %collective-permute-start.37 = (bf16[4,64,2304]{2,1,0:T(8,128)(2,1)}, bf16[4,64,2304]{2,1,0:T(8,128)(2,1)}, u32[]{:S(2)}, u32[]{:S(2)}) collective-permute-start(bf16[4,64,2304]{2,1,0:T(8,128)(2,1)} %fusion.74), channel_id=1, source_target_pairs={{0,1},{1,0},{2,3},{3,2},{4,5},{5,4},{6,7},{7,6},{8,9},{9,8},{10,11... | collective-permute-start | bytes 3538952 | tf_op jit(solution)/shard_map/ppermute | solution.py:204
  377.5 27.9 %collective-permute-start.44 = (bf16[3,96,2304]{2,1,0:T(8,128)(2,1)}, bf16[3,96,2304]{2,1,0:T(8,128)(2,1)}, u32[]{:S(2)}, u32[]{:S(2)}) collective-permute-start(bf16[3,96,2304]{2,1,0:T(8,128)(2,1)} %collective-permute-done.43), channel_id=1, source_target_pairs={{0,8},{8,0},{16,24},{24,16},{1,9},{9,1},{17,25},{25,17},{2,10},{10... | collective-permute-start | bytes 3981320 | tf_op jit(solution)/shard_map/ppermute | solution.py:198
  381.1 49.7 %collective-permute-start.42 = (bf16[576,1152]{1,0:T(8,128)(2,1)}, bf16[576,1152]{1,0:T(8,128)(2,1)}, u32[]{:S(2)}, u32[]{:S(2)}) collective-permute-start(bf16[576,1152]{1,0:T(8,128)(2,1)} %get-tuple-element.67), channel_id=1, source_target_pairs={{0,1},{1,0},{2,3},{3,2},{4,5},{5,4},{6,7},{7,6},{8,9},{9,8},{10,11... | collective-permute-start | bytes 3981320 | tf_op jit(solution)/shard_map/ppermute | solution.py:204
  405.4 388.5 %reduce-scatter.11.cloned.1.call-start = ((), (), s32[]{:S(2)}) async-start(), calls=%async_computation.7 | async-start | bytes 6635520 | tf_op jit(solution)/shard_map/reduce_scatter | solution.py:230
  442.6 354.2 %reduce-scatter.9.cloned.1.call-start = ((), (), s32[]{:S(2)}) async-start(), calls=%async_computation.6 | async-start | bytes 6635520 | tf_op jit(solution)/shard_map/reduce_scatter | solution.py:230
  442.7 31.1 %collective-permute-start.39 = (bf16[3,96,2304]{2,1,0:T(8,128)(2,1)}, bf16[3,96,2304]{2,1,0:T(8,128)(2,1)}, u32[]{:S(2)}, u32[]{:S(2)}) collective-permute-start(bf16[3,96,2304]{2,1,0:T(8,128)(2,1)} %copy-done.48), channel_id=1, source_target_pairs={{0,1},{1,0},{2,3},{3,2},{4,5},{5,4},{6,7},{7,6},{8,9},{9,8},{10,11... | collective-permute-start | bytes 3981320 | tf_op jit(solution)/shard_map/ppermute | solution.py:204
  474.3 17.3 %collective-permute-start.17 = (bf16[3,48,2304]{2,1,0:T(8,128)(2,1)S(1)}, bf16[3,48,2304]{2,1,0:T(8,128)(2,1)S(1)}, u32[]{:S(2)}, u32[]{:S(2)}) collective-permute-start(bf16[3,48,2304]{2,1,0:T(8,128)(2,1)S(1)} %copy-done.26), channel_id=1, source_target_pairs={{0,16},{8,24},{16,0},{24,8},{1,17},{9,25},{17,1},{25,9},{2,18},{10... | collective-permute-start | bytes 1990664 | tf_op jit(solution)/shard_map/ppermute | solution.py:201
  477.7 32.0 %collective-permute-start.41 = (bf16[576,1152]{1,0:T(8,128)(2,1)S(1)}, bf16[576,1152]{1,0:T(8,128)(2,1)S(1)}, u32[]{:S(2)}, u32[]{:S(2)}) collective-permute-start(bf16[576,1152]{1,0:T(8,128)(2,1)S(1)} %get-tuple-element.69), channel_id=1, source_target_pairs={{0,1},{1,0},{2,3},{3,2},{4,5},{5,4},{6,7},{7,6},{8,9},{9,8},{10,11... | collective-permute-start | bytes 3981320 | tf_op jit(solution)/shard_map/ppermute | solution.py:204
  492.8 27.4 %collective-permute-start.18 = (bf16[3,96,2304]{2,1,0:T(8,128)(2,1)}, bf16[3,96,2304]{2,1,0:T(8,128)(2,1)}, u32[]{:S(2)}, u32[]{:S(2)}) collective-permute-start(bf16[3,96,2304]{2,1,0:T(8,128)(2,1)} %pad_maximum_fusion.18), channel_id=1, source_target_pairs={{0,8},{8,0},{16,24},{24,16},{1,9},{9,1},{17,25},{25,17},{2,10},{10... | collective-permute-start | bytes 3981320 | tf_op jit(solution)/shard_map/ppermute | solution.py:198
  494.5 74.2 %collective-permute-start.38 = (bf16[576,1152]{1,0:T(8,128)(2,1)}, bf16[576,1152]{1,0:T(8,128)(2,1)}, u32[]{:S(2)}, u32[]{:S(2)}) collective-permute-start(bf16[576,1152]{1,0:T(8,128)(2,1)} %get-tuple-element.71), channel_id=1, source_target_pairs={{0,1},{1,0},{2,3},{3,2},{4,5},{5,4},{6,7},{7,6},{8,9},{9,8},{10,11... | collective-permute-start | bytes 3981320 | tf_op jit(solution)/shard_map/ppermute | solution.py:204
  520.2 279.7 %reduce-scatter.7.cloned.1.call-start = ((), (), s32[]{:S(2)}) async-start(), calls=%async_computation.5 | async-start | bytes 6635520 | tf_op jit(solution)/shard_map/reduce_scatter | solution.py:230
  567.8 52.7 %collective-permute-start.25 = (bf16[4,3,192,512]{3,2,1,0:T(8,128)(2,1)}, bf16[4,3,192,512]{3,2,1,0:T(8,128)(2,1)}, u32[]{:S(2)}, u32[]{:S(2)}) collective-permute-start(bf16[4,3,192,512]{3,2,1,0:T(8,128)(2,1)} %fusion.34), channel_id=1, source_target_pairs={{0,1},{1,0},{2,3},{3,2},{4,5},{5,4},{6,7},{7,6},{8,9},{9,8},{10,11... | collective-permute-start | bytes 7077896 | tf_op jit(solution)/shard_map/ppermute | solution.py:204
  623.3 38.9 %collective-permute-start.26 = (bf16[3,192,512]{2,1,0:T(8,128)(2,1)S(1)}, bf16[3,192,512]{2,1,0:T(8,128)(2,1)S(1)}, u32[]{:S(2)}, u32[]{:S(2)}) collective-permute-start(bf16[3,192,512]{2,1,0:T(8,128)(2,1)S(1)} %get-tuple-element.76), channel_id=1, source_target_pairs={{2,0},{3,1},{4,2},{5,3},{6,4},{7,5},{10,8},{11,9},{12,10},{13,11},... | collective-permute-start | bytes 1769480 | tf_op jit(solution)/shard_map/ppermute | solution.py:208
  624.6 113.3 %collective-permute-start.27 = (bf16[3,192,512]{2,1,0:T(8,128)(2,1)S(1)}, bf16[3,192,512]{2,1,0:T(8,128)(2,1)S(1)}, u32[]{:S(2)}, u32[]{:S(2)}) collective-permute-start(bf16[3,192,512]{2,1,0:T(8,128)(2,1)S(1)} %get-tuple-element.78), channel_id=1, source_target_pairs={{4,0},{5,1},{6,2},{7,3},{12,8},{13,9},{14,10},{15,11},{20,16},{21,... | collective-permute-start | bytes 1769480 | tf_op jit(solution)/shard_map/ppermute | solution.py:208
  625.9 112.0 %collective-permute-start.28 = (bf16[3,192,512]{2,1,0:T(8,128)(2,1)S(1)}, bf16[3,192,512]{2,1,0:T(8,128)(2,1)S(1)}, u32[]{:S(2)}, u32[]{:S(2)}) collective-permute-start(bf16[3,192,512]{2,1,0:T(8,128)(2,1)S(1)} %get-tuple-element.77), channel_id=1, source_target_pairs={{6,0},{7,1},{14,8},{15,9},{22,16},{23,17},{30,24},{31,25}} | collective-permute-start | bytes 1769480 | tf_op jit(solution)/shard_map/ppermute | solution.py:208
  765.3 15.2 %collective-permute-start.35 = (bf16[2,192,128]{2,1,0:T(8,128)(2,1)S(1)}, bf16[2,192,128]{2,1,0:T(8,128)(2,1)S(1)}, u32[]{:S(2)}, u32[]{:S(2)}) collective-permute-start(bf16[2,192,128]{2,1,0:T(8,128)(2,1)S(1)} %get-tuple-element.119), channel_id=1, source_target_pairs={{0,4},{1,5},{2,6},{3,7},{4,0},{5,1},{6,2},{7,3},{8,12},{9,13},{10,... | collective-permute-start | bytes 294920 | tf_op jit(solution)/shard_map/ppermute | solution.py:211
  765.4 15.1 %collective-permute-start.36 = (bf16[2,192,128]{2,1,0:T(8,128)(2,1)S(1)}, bf16[2,192,128]{2,1,0:T(8,128)(2,1)S(1)}, u32[]{:S(2)}, u32[]{:S(2)}) collective-permute-start(bf16[2,192,128]{2,1,0:T(8,128)(2,1)S(1)} %get-tuple-element.120), channel_id=1, source_target_pairs={{0,6},{1,7},{2,0},{3,1},{4,2},{5,3},{6,4},{7,5},{8,14},{9,15},{10,... | collective-permute-start | bytes 294920 | tf_op jit(solution)/shard_map/ppermute | solution.py:211
  (152 other events, 1529.8 us)
Sparse Core Ops, SparseCore 0:
  405.5 44.8 reduce-scatter.4
  452.7 100.5 reduce-scatter.10
  555.7 99.5 reduce-scatter.8
  657.4 131.6 reduce-scatter.6
